TPU v7x, 128 devices: a whole 4x4x4 slice. The times are simulated.
128 devices in a mesh: row: 16 (over x, z), col: 8 (over y, core).
Axes of the slice: x: 4, y: 4, z: 4, core: 2. Of those that a mesh axis runs over, the one named last changes fastest.
Arguments:
- currents: bfloat16 [256, 128, 512], P('row', 'col'), may hold values from -6 to 6
- counts: int32 [256, 128], P('row', 'col'), may hold values from 0 to 16
- radiate: bfloat16 [512, 1024], replicated, may hold values from -0.25 to 0.25
- receive: bfloat16 [1024, 512], replicated, may hold values from -0.1875 to 0.1875
- near_blocks: bfloat16 [9, 512, 512], replicated, may hold values from -0.09375 to 0.09375
- translate: float32 [4, 49, 1024], replicated, may hold values from -0.84 to 0.84
- shift: float32 [3, 4, 1024], replicated, may hold values from -3 to 3
Outputs:
- field: bfloat16 [256, 128, 512], P('row', 'col')
Inputs may be any that keep to these rules, and one draw needn't show every extreme that they name: `counts`: atoms present in each leaf box; they occupy its first slots.
All inputs are finite; a program needn't handle non-finite values.
Results may differ from a plain program's by a relative error of at most 0.017.
Values may be sent and summed in bfloat16 or wider, within the bound.
No kernel may reach another device: no remote copies, remote signals or barrier semaphores. Data moves between devices by JAX's collectives and lax.ppermute only.
A program may use at most 192 MiB of HBM per device.

v0:
```python
import functools

import jax
import jax.numpy as jnp
from jax import lax
from jax.experimental import pallas as pl
from jax.experimental.pallas import tpu as pltpu
from jax.sharding import PartitionSpec as P

U = 16
INTERPRET = False
F32 = jnp.float32
BF16 = jnp.bfloat16
N0 = 16
ROW0 = 32
ROWS = 24
SX = 72
SY = 48
OFFS = [(dx, dy) for dx in range(-3, 4) for dy in range(-3, 4) if max(abs(dx), abs(dy)) >= 2]


def lanes(c):
    return slice(c * 128, (c + 1) * 128)


def occupied_rows(cnt_ref, x):
    row = cnt_ref[x : x + 1, :].astype(F32)
    one = lax.broadcasted_iota(jnp.int32, (N0, N0), 0) == lax.broadcasted_iota(jnp.int32, (N0, N0), 1)
    count = jnp.sum(jnp.where(one, jnp.broadcast_to(row, (N0, N0)), 0.0), axis=1, keepdims=True)
    lane = lax.broadcasted_iota(jnp.int32, (N0, 512), 1).astype(F32)
    return lane < count * float(2 * U)


def swap_perm(count, odd):
    pairs = [(i, i + 1) for i in range(odd, count - 1, 2)]
    if odd:
        pairs.append((count - 1, 0))
    return pairs + [(b, a) for a, b in pairs]


def upward(cur, cnt, rad, shf, msk, p0, p1, p2, p3, m_even, m_odd, c0, f0, me, mo):
    even = (lax.axis_index("col") % 2) == 0
    for x in range(N0):
        kept = jnp.where(occupied_rows(cnt, x), cur[x].astype(F32), 0.0)
        msk[x] = kept.astype(BF16)
        for c in range(4):
            c0[c, x * 16 : (x + 1) * 16, :] = kept[:, lanes(c)]
    lhs = msk[...].reshape(N0 * N0, 512)
    for n in range(4):
        out = jnp.dot(lhs, rad[:, n * 256 : (n + 1) * 256], preferred_element_type=F32).astype(BF16)
        for h in range(2):
            p0[2 * n + h] = out[:, lanes(h)]
            f0[2 * n + h] = out[:, lanes(h)].astype(F32)
    source, rows = f0, 16
    for level, (dest, size) in enumerate(((p1, 8), (p2, 4), (p3, 2))):
        for i in range(size):
            for c in range(4):
                re = im = None
                for a in range(2):
                    for b in range(2):
                        at = pl.ds((2 * i + a) * rows + b, size, stride=2)
                        s_re = source[c, at, :]
                        s_im = source[4 + c, at, :]
                        t_re = shf[level, 2 * a + b : 2 * a + b + 1, lanes(c)]
                        t_im = shf[level, 2 * a + b : 2 * a + b + 1, lanes(4 + c)]
                        q_re = t_re * s_re - t_im * s_im
                        q_im = t_re * s_im + t_im * s_re
                        re = q_re if re is None else re + q_re
                        im = q_im if im is None else im + q_im
                dest[c, i * 8 : i * 8 + size, :] = re.astype(BF16).astype(F32)
                dest[4 + c, i * 8 : i * 8 + size, :] = im.astype(BF16).astype(F32)
        source, rows = dest, 8

    def put(c, at, lo, hi):
        me[c, at, :] = jnp.where(even, hi, lo)
        mo[c, at, :] = jnp.where(even, lo, hi)

    for r in range(2):
        for c in range(4):
            lo = c0[c, pl.ds(r, 16, stride=16), :]
            hi = c0[c, pl.ds(14 + r, 16, stride=16), :]
            for h in range(2):
                put(c + 4 * h, pl.ds(r, 8, stride=2), lo[8 * h : 8 * h + 8], hi[8 * h : 8 * h + 8])
        for c in range(8):
            put(c, pl.ds(16 + r, 8, stride=2), p1[c, pl.ds(r, 8, stride=8), :], p1[c, pl.ds(6 + r, 8, stride=8), :])
            put(c, pl.ds(32 + r, 4, stride=2), p2[c, pl.ds(r, 4, stride=8), :], p2[c, pl.ds(2 + r, 4, stride=8), :])
            both = p3[c, pl.ds(r, 2, stride=8), :]
            put(c, pl.ds(40 + r, 2, stride=2), both, both)
    for c in range(8):
        me[c, 44:48, :] = jnp.zeros((4, 128), F32)
        mo[c, 44:48, :] = jnp.zeros((4, 128), F32)
        m_even[c] = me[c].astype(BF16)
        m_odd[c] = mo[c].astype(BF16)


def received(axis, r_even, r_odd, lo, hi):
    me = lax.axis_index(axis)
    last = lax.axis_size(axis) - 1
    even = (me % 2) == 0
    for c in range(8):
        from_even = r_even[c].astype(F32)
        from_odd = r_odd[c].astype(F32)
        lo[c] = jnp.where(me == 0, 0.0, jnp.where(even, from_odd, from_even))
        hi[c] = jnp.where(me == last, 0.0, jnp.where(even, from_even, from_odd))


def strips(r_even, r_odd, msk, p1, p2, p3, x_even, x_odd, ylo, yhi, mlo, mhi):
    received("col", r_even, r_odd, ylo, yhi)
    even = (lax.axis_index("row") % 2) == 0
    for dest, first in ((mlo, 0), (mhi, 1)):
        for xr in range(2):
            x = 14 * first + xr
            kept = msk[x].astype(F32)
            for c in range(4):
                dest[4 * xr + c, 2:18, :] = kept[:, lanes(c)]
                at = slice(2 * (x % 8), 2 * (x % 8) + 2)
                dest[4 * xr + c, 0:2, :] = ylo[c + 4 * (x // 8), at, :]
                dest[4 * xr + c, 18:20, :] = yhi[c + 4 * (x // 8), at, :]
            for c in range(8):
                for level_ref, size, base, inside in ((p1, 8, 32, 16), (p2, 4, 56, 32), (p3, 2, 20, 40)):
                    x = (size - 2) * first + xr
                    at = base + (size + 4) * xr
                    dest[c, at + 2 : at + 2 + size, :] = level_ref[c, x * 8 : x * 8 + size, :]
                    dest[c, at : at + 2, :] = ylo[c, inside + 2 * x : inside + 2 * x + 2, :]
                    dest[c, at + 2 + size : at + 4 + size, :] = yhi[c, inside + 2 * x : inside + 2 * x + 2, :]
    for c in range(8):
        lo = mlo[c]
        hi = mhi[c]
        x_even[c] = jnp.where(even, hi, lo).astype(BF16)
        x_odd[c] = jnp.where(even, lo, hi).astype(BF16)


def twice(ref, m, at):
    return jnp.concatenate([ref[2 * m, at, :], ref[2 * m + 1, at, :]], axis=0)


def parity_rows():
    return (lax.broadcasted_iota(jnp.int32, (16, 128), 0) % 2) == 0


def factor_tile(tr, level, offset, m):
    dx, dy = offset
    row = (dx + 3) * 7 + dy + 3
    low = jnp.broadcast_to(tr[level, row : row + 1, lanes(2 * m)], (8, 128))
    high = jnp.broadcast_to(tr[level, row : row + 1, lanes(2 * m + 1)], (8, 128))
    return jnp.concatenate([low, high], axis=0)


def add_product(part, factor, value):
    t_re, t_im = factor
    v_re, v_im = value
    re = t_re * v_re - t_im * v_im
    im = t_re * v_im + t_im * v_re
    return (re, im) if part is None else (part[0] + re, part[1] + im)


def add_part(total, part):
    re, im = part[0].astype(F32), part[1].astype(F32)
    return (re, im) if total is None else (total[0] + re, total[1] + im)


def leaf_far(sk, tt, inc, first, last):
    for m in range(2):

        def body(i, carry):
            total = {}
            for pair in range(3):
                part = {}
                for xs in (2 * pair, 2 * pair + 1):
                    for k in range(6):
                        if xs in (2, 3) and k in (2, 3):
                            continue
                        value = (sk[k, 2 * i + xs, m], sk[k, 2 * i + xs, 2 + m])
                        for a in range(2):
                            for b in range(2):
                                offset = (xs - 2 - a, k - 2 - b)
                                if offset not in OFFS:
                                    continue
                                o = OFFS.index(offset)
                                part[a, b] = add_product(part.get((a, b)), (tt[o, m], tt[o, 2 + m]), value)
                for key in part:
                    total[key] = add_part(total.get(key), part[key])
            for (a, b), sums in total.items():
                for q in range(2):
                    for h in range(2):
                        inc[4 * q + 2 * m + h, pl.ds((2 * i + a) * 16 + b, 8, stride=2), :] = sums[q][8 * h : 8 * h + 8]
            return carry

        lax.fori_loop(first, last, body, 0)


def slots_of(dx):
    full = [(k, k - 2, k - 3) for k in range(6)]
    return full if abs(dx) >= 2 else [full[0], full[5], (6, 2, -2)]


SLOTS = [(dx, slot) for dx in range(-3, 4) for slot in slots_of(dx)]


def level_tables(tr, level, ts):
    rows = parity_rows()
    for s, (dx, (_, dy_even, dy_odd)) in enumerate(SLOTS):
        for m in range(4):
            tile = jnp.where(rows, factor_tile(tr, level, (dx, dy_even), m), factor_tile(tr, level, (dx, dy_odd), m))
            ts[s, m] = tile.astype(BF16)


def level_sources(fx, sk, xes):
    rows = parity_rows()
    for xe in xes:
        for m in range(4):
            views = [twice(fx, m, slice(xe * ROWS + 6 + d, xe * ROWS + 14 + d)) for d in range(-1, 6)]
            for k in range(6):
                sk[k, xe, m] = jnp.where(rows, views[k + 1], views[k]).astype(BF16)
            sk[6, xe, m] = jnp.where(rows, views[5], views[1]).astype(BF16)


def level_far(sk, ts, inc, size):
    for i in range(size // 2):
        for a in range(2):
            for m in range(2):
                total = None
                for pair in range(3):
                    part = None
                    for xs in (2 * pair, 2 * pair + 1):
                        dx = xs - 2 - a
                        for slot in slots_of(dx):
                            s = SLOTS.index((dx, slot))
                            value = (sk[slot[0], 2 * i + xs, m], sk[slot[0], 2 * i + xs, 2 + m])
                            part = add_product(part, (ts[s, m], ts[s, 2 + m]), value)
                    total = add_part(total, part)
                x = 2 * i + a
                for q in range(2):
                    for h in range(2):
                        inc[4 * q + 2 * m + h, x * 8 : x * 8 + size, :] = total[q][8 * h : 8 * h + size]


def add_parent(inc, parent, shf, level, size, rows):
    half = size // 2
    for x in range(size):
        for b in range(2):
            row = 2 * (x % 2) + b
            at = pl.ds(x * rows + b, half, stride=2)
            for c in range(4):
                q_re = parent[c, (x // 2) * 8 : (x // 2) * 8 + half, :]
                q_im = parent[4 + c, (x // 2) * 8 : (x // 2) * 8 + half, :]
                t_re = shf[level, row : row + 1, lanes(c)]
                t_im = shf[level, row : row + 1, lanes(4 + c)]
                inc[c, at, :] = inc[c, at, :] + (t_re * q_re + t_im * q_im)
                inc[4 + c, at, :] = inc[4 + c, at, :] + (t_re * q_im - t_im * q_re)


def downward(
    cnt, msk, p0, p1, p2, p3, r_even, r_odd, x_even, x_odd, rad, rec, near, tr, shf, field,
    ylo, yhi, xlo, xhi, cx, ln, f0, res, sk0, tt, f1, f2, f3, sk1, sk2, sk3, ts, inc0, inc1, inc2, inc3, half,
):
    received("col", r_even, r_odd, ylo, yhi)
    received("row", x_even, x_odd, xlo, xhi)
    for x in range(N0):
        kept = msk[x].astype(F32)
        base = (x + 2) * ROW0
        at = slice(2 * (x % 8), 2 * (x % 8) + 2)
        for c in range(4):
            cx[c, base + 8 : base + 24, :] = kept[:, lanes(c)]
            cx[c, base + 6 : base + 8, :] = ylo[c + 4 * (x // 8), at, :]
            cx[c, base + 24 : base + 26, :] = yhi[c + 4 * (x // 8), at, :]
    for src, xe in ((xlo, 0), (xhi, 18)):
        for xr in range(2):
            for c in range(4):
                cx[c, (xe + xr) * ROW0 + 6 : (xe + xr) * ROW0 + 26, :] = src[4 * xr + c, 0:20, :]
    for xi in range(18):
        for dy in range(-1, 2):
            for c in range(4):
                at = (xi + 1) * ROW0 + 8 + dy
                ln[xi, :, (dy + 1) * 512 + c * 128 : (dy + 1) * 512 + (c + 1) * 128] = cx[c, at : at + 16, :].astype(BF16)
    near_sum = None
    for dx in range(3):
        left = ln[dx : dx + 16].reshape(N0 * N0, 1536)
        for dy in range(3):
            term = jnp.dot(left[:, dy * 512 : (dy + 1) * 512], near[3 * dx + dy], preferred_element_type=F32)
            near_sum = term if near_sum is None else near_sum + term
    sides = [jnp.concatenate([src[4 * h + c, 0:16, :] for c in range(4)], axis=1) for src in (ylo, yhi) for h in range(2)]
    for xe in (0, 1, 18, 19):
        sides.append(jnp.concatenate([cx[c, xe * ROW0 : (xe + 1) * ROW0, :] for c in range(4)], axis=1))
    halo = jnp.dot(jnp.concatenate(sides, axis=0).astype(BF16), rad[...], preferred_element_type=F32)
    halo = halo.astype(BF16).astype(F32)
    for c in range(8):
        res[c] = halo[0:64, lanes(c)]
        for n, xe in enumerate((0, 1, 18, 19)):
            f0[c, xe * ROW0 : (xe + 1) * ROW0, :] = halo[64 + 32 * n : 96 + 32 * n, lanes(c)]
        for x in range(N0):
            base = (x + 2) * ROW0
            at = 16 * (x // 8) + 2 * (x % 8)
            f0[c, base + 8 : base + 24, :] = p0[c, x * 16 : (x + 1) * 16, :].astype(F32)
            f0[c, base + 6 : base + 8, :] = res[c, at : at + 2, :]
            f0[c, base + 24 : base + 26, :] = res[c, 32 + at : 34 + at, :]
    for xe in range(20):
        for k in range(6):
            for m in range(4):
                sk0[k, xe, m] = twice(f0, m, pl.ds(xe * ROW0 + 6 + k, 8, stride=2)).astype(BF16)
    for o, offset in enumerate(OFFS):
        for m in range(4):
            tt[o, m] = factor_tile(tr, 0, offset, m).astype(BF16)
    leaf_far(sk0, tt, inc0, 0, 8)

    above = ((f1, sk1, inc1, p1, 8, 32, 16), (f2, sk2, inc2, p2, 4, 56, 32), (f3, sk3, inc3, p3, 2, 20, 40))
    for level, (fx, sk, inc, own, size, x_base, y_base) in enumerate(above, 1):
        for c in range(8):
            for x in range(size):
                base = (x + 2) * ROWS
                fx[c, base + 8 : base + 8 + size, :] = own[c, x * 8 : x * 8 + size, :]
                fx[c, base + 6 : base + 8, :] = ylo[c, y_base + 2 * x : y_base + 2 * x + 2, :]
                fx[c, base + 8 + size : base + 10 + size, :] = yhi[c, y_base + 2 * x : y_base + 2 * x + 2, :]
            for src, xe in ((xlo, 0), (xhi, size + 2)):
                for xr in range(2):
                    at = x_base + (size + 4) * xr
                    fx[c, (xe + xr) * ROWS + 6 : (xe + xr) * ROWS + 10 + size, :] = src[c, at : at + size + 4, :]
        level_tables(tr, level, ts)
        level_sources(fx, sk, range(size + 4))
        level_far(sk, ts, inc, size)
    add_parent(inc2, inc3, shf, 2, 4, 8)
    add_parent(inc1, inc2, shf, 1, 8, 8)
    add_parent(inc0, inc1, shf, 0, 16, 16)
    for c in range(8):
        half[:, lanes(c)] = inc0[c].astype(BF16)
    total = near_sum + jnp.dot(half[...], rec[...], preferred_element_type=F32)
    for x in range(N0):
        field[x] = jnp.where(occupied_rows(cnt, x), total[x * 16 : (x + 1) * 16], 0.0).astype(BF16)


def call(kernel, outs, scratch, *args):
    return pl.pallas_call(
        kernel,
        out_shape=outs,
        scratch_shapes=scratch,
        compiler_params=pltpu.CompilerParams(vmem_limit_bytes=56 * 1024 * 1024),
        interpret=INTERPRET,
    )(*args)


def shape(dims, kind):
    return jax.ShapeDtypeStruct(dims, kind)


def swap(value, axis, odd):
    return lax.ppermute(value, axis, swap_perm(lax.axis_size(axis), odd))


def shards(currents, counts, radiate, receive, near_blocks, translate, shift):
    mem = pltpu.VMEM
    masked, p0, p1, p2, p3, m_even, m_odd = call(
        upward,
        [
            shape((16, 16, 512), BF16),
            shape((8, 256, 128), BF16),
            shape((8, 64, 128), F32),
            shape((8, 32, 128), F32),
            shape((8, 16, 128), F32),
            shape((8, SY, 128), BF16),
            shape((8, SY, 128), BF16),
        ],
        [mem((4, 256, 128), F32), mem((8, 256, 128), F32), mem((8, SY, 128), F32), mem((8, SY, 128), F32)],
        currents, counts, radiate, shift,
    )
    r_even = swap(m_even, "col", 0)
    r_odd = swap(m_odd, "col", 1)
    s_even, s_odd = call(
        strips,
        [shape((8, SX, 128), BF16)] * 2,
        [mem((8, SY, 128), F32)] * 2 + [mem((8, SX, 128), F32)] * 2,
        r_even, r_odd, masked, p1, p2, p3,
    )
    x_even = swap(s_even, "row", 0)
    x_odd = swap(s_odd, "row", 1)
    return call(
        downward,
        shape((16, 16, 512), BF16),
        [
            mem((8, SY, 128), F32), mem((8, SY, 128), F32), mem((8, SX, 128), F32), mem((8, SX, 128), F32),
            mem((4, 20 * ROW0, 128), F32), mem((18, 16, 1536), BF16),
            mem((8, 20 * ROW0, 128), F32), mem((8, 64, 128), F32),
            mem((6, 20, 4, 16, 128), BF16), mem((40, 4, 16, 128), BF16),
            mem((8, 12 * ROWS, 128), F32), mem((8, 8 * ROWS, 128), F32), mem((8, 6 * ROWS, 128), F32),
            mem((7, 12, 4, 16, 128), BF16), mem((7, 8, 4, 16, 128), BF16), mem((7, 6, 4, 16, 128), BF16),
            mem((33, 4, 16, 128), BF16),
            mem((8, 256, 128), F32), mem((8, 64, 128), F32), mem((8, 32, 128), F32), mem((8, 16, 128), F32),
            mem((256, 1024), BF16),
        ],
        counts, masked, p0, p1, p2, p3, r_even, r_odd, x_even, x_odd, radiate, receive, near_blocks, translate, shift,
    )


def solution(mesh):
    return jax.shard_map(
        shards,
        mesh=mesh,
        in_specs=(P("row", "col", None), P("row", "col"), P(), P(), P(), P(), P()),
        out_specs=P("row", "col", None),
        check_vma=False,
    )
```

profile of v0, /device:TPU:25, one launch (start us, length us, event | category | flops | bytes accessed | tf_op | source)
XLA Modules:
  0.0 38.7 jit_solution(4912400436675026866)
XLA Ops:
  0.0 3.2 %shard_map.73 = (bf16[16,16,512]{2,1,0:T(8,128)(2,1)}, bf16[8,256,128]{2,1,0:T(8,128)(2,1)}, f32[8,64,128]{2,1,0:T(8,128)}, f32[8,32,128]{2,1,0:T(8,128)}, f32[8...) custom-call(bf16[16,16,512]{2,1,0:T(8,128)(2,1)} %cur.1, s32[16,16]{1,0:T(8,128)} %cnt.3, ...), custom_call_target="tpu_custom_call" | custom-call | tf_op jit(solution)/shard_map/pallas_call | solution.py:332
  3.2 0.7 %collective-permute-start = (bf16[8,48,128]{2,1,0:T(8,128)(2,1)}, bf16[8,48,128]{2,1,0:T(8,128)(2,1)S(1)}, u32[]{:S(2)}, u32[]{:S(2)}) collective-permute-start(bf16[8,48,128]{2,1,0:T(8,128)(2,1)} %get-tuple-element.19), channel_id=1, source_target_pairs={{0,1},{2,3},{4,5},{6,7},{1,0},{3,2},{5,4},{7,6},{8,9},{10,11},{12,... | collective-permute-start | bytes 294920 | tf_op jit(solution)/shard_map/ppermute | solution.py:346
  3.9 0.0 collective-permute-start.1
  3.9 1.2 %collective-permute-done.r_even = bf16[8,48,128]{2,1,0:T(8,128)(2,1)S(1)} collective-permute-done((bf16[8,48,128]{2,1,0:T(8,128)(2,1)}, bf16[8,48,128]{2,1,0:T(8,128)(2,1)S(1)}, u32[]{:S(2)}, u32[]{:S(2)}) %collective-permute-start) | collective-permute-done | bytes 98336 | tf_op jit(solution)/shard_map/ppermute | solution.py:346
  5.0 0.0 copy-start
  5.0 4.3 %collective-permute-done.1.r_odd = bf16[8,48,128]{2,1,0:T(8,128)(2,1)S(1)} collective-permute-done((bf16[8,48,128]{2,1,0:T(8,128)(2,1)}, bf16[8,48,128]{2,1,0:T(8,128)(2,1)S(1)}, u32[]{:S(2)}, u32[]{:S(2)}) %collective-permute-start.1) | collective-permute-done | bytes 98336 | tf_op jit(solution)/shard_map/ppermute | solution.py:346
  9.3 0.0 copy-start.1
  9.3 0.0 copy-done
  9.3 0.6 %copy-done.1 = bf16[8,48,128]{2,1,0:T(8,128)(2,1)} copy-done((bf16[8,48,128]{2,1,0:T(8,128)(2,1)}, bf16[8,48,128]{2,1,0:T(8,128)(2,1)S(1)}, u32[]{:S(2)}) %copy-start.1) | copy-done | bytes 98328
  10.0 2.0 %shard_map.74 = (bf16[8,72,128]{2,1,0:T(8,128)(2,1)}, bf16[8,72,128]{2,1,0:T(8,128)(2,1)}) custom-call(bf16[8,48,128]{2,1,0:T(8,128)(2,1)} %copy-done, bf16[8,48,128]{2,1,0:T(8,128)(2,1)} %copy-done.1, bf16[16,16,512]{2,1,0:T(8,128)(2,1)} %get-tuple-element.14.msk, f32[8,64,128]{2,1,0:T(8,128)} %get-tuple-element.16.p1, f32[8,32,128]{2,1,0:T(8,128)} %get-tuple-element.17.p2, ...), custom_call_target="tpu_custom_call" | custom-call | tf_op jit(solution)/shard_map/pallas_call | solution.py:332
  12.0 1.6 %collective-permute-start.2 = (bf16[8,72,128]{2,1,0:T(8,128)(2,1)}, bf16[8,72,128]{2,1,0:T(8,128)(2,1)S(1)}, u32[]{:S(2)}, u32[]{:S(2)}) collective-permute-start(bf16[8,72,128]{2,1,0:T(8,128)(2,1)} %get-tuple-element.21), channel_id=1, source_target_pairs={{0,8},{16,24},{32,40},{48,56},{64,72},{80,88},{96,104},{112,120},{... | collective-permute-start | bytes 442376 | tf_op jit(solution)/shard_map/ppermute | solution.py:346
  13.6 4.4 %collective-permute-start.3 = (bf16[8,72,128]{2,1,0:T(8,128)(2,1)}, bf16[8,72,128]{2,1,0:T(8,128)(2,1)S(1)}, u32[]{:S(2)}, u32[]{:S(2)}) collective-permute-start(bf16[8,72,128]{2,1,0:T(8,128)(2,1)} %get-tuple-element.22), channel_id=1, source_target_pairs={{8,16},{24,32},{40,48},{56,64},{72,80},{88,96},{104,112},{120,0},{... | collective-permute-start | bytes 442376 | tf_op jit(solution)/shard_map/ppermute | solution.py:346
  18.1 2.5 %copy.8.tr = f32[4,49,1024]{2,1,0:T(8,128)} copy(f32[4,49,1024]{2,0,1:T(4,128)} %param.12) | data formatting | bytes 1605632 | tf_op args[5]
  20.6 0.0 collective-permute-done.2.x_even
  20.6 0.0 copy-start.2
  20.6 1.7 %collective-permute-done.3.x_odd = bf16[8,72,128]{2,1,0:T(8,128)(2,1)S(1)} collective-permute-done((bf16[8,72,128]{2,1,0:T(8,128)(2,1)}, bf16[8,72,128]{2,1,0:T(8,128)(2,1)S(1)}, u32[]{:S(2)}, u32[]{:S(2)}) %collective-permute-start.3) | collective-permute-done | bytes 147488 | tf_op jit(solution)/shard_map/ppermute | solution.py:346
  22.3 0.0 copy-start.3
  22.3 0.0 copy-done.2
  22.3 0.6 %copy-done.3 = bf16[8,72,128]{2,1,0:T(8,128)(2,1)} copy-done((bf16[8,72,128]{2,1,0:T(8,128)(2,1)}, bf16[8,72,128]{2,1,0:T(8,128)(2,1)S(1)}, u32[]{:S(2)}) %copy-start.3) | copy-done | bytes 147480
  23.0 15.7 %shard_map.75 = bf16[16,16,512]{2,1,0:T(8,128)(2,1)} custom-call(s32[16,16]{1,0:T(8,128)} %cnt.3, bf16[16,16,512]{2,1,0:T(8,128)(2,1)} %get-tuple-element.14.msk, bf16[8,256,128]{2,1,0:T(8,128)(2,1)} %get-tuple-element.15.p0, f32[8,64,128]{2,1,0:T(8,128)} %get-tuple-element.16.p1, f32[8,32,128]{2,1,0:T(8,128)} %get-tuple-element.17.p2, ...), custom_call_target="tpu_custom_call" | custom-call | tf_op jit(solution)/shard_map/pallas_call | solution.py:332
Async XLA Ops:
  3.2 1.8 %collective-permute-start = (bf16[8,48,128]{2,1,0:T(8,128)(2,1)}, bf16[8,48,128]{2,1,0:T(8,128)(2,1)S(1)}, u32[]{:S(2)}, u32[]{:S(2)}) collective-permute-start(bf16[8,48,128]{2,1,0:T(8,128)(2,1)} %get-tuple-element.19), channel_id=1, source_target_pairs={{0,1},{2,3},{4,5},{6,7},{1,0},{3,2},{5,4},{7,6},{8,9},{10,11},{12,... | collective-permute-start | bytes 294920 | tf_op jit(solution)/shard_map/ppermute | solution.py:346
  3.9 5.5 %collective-permute-start.1 = (bf16[8,48,128]{2,1,0:T(8,128)(2,1)}, bf16[8,48,128]{2,1,0:T(8,128)(2,1)S(1)}, u32[]{:S(2)}, u32[]{:S(2)}) collective-permute-start(bf16[8,48,128]{2,1,0:T(8,128)(2,1)} %get-tuple-element.20), channel_id=1, source_target_pairs={{1,2},{3,4},{5,6},{7,0},{2,1},{4,3},{6,5},{0,7},{9,10},{11,12},{13... | collective-permute-start | bytes 294920 | tf_op jit(solution)/shard_map/ppermute | solution.py:346
  5.0 4.3 %copy-start = (bf16[8,48,128]{2,1,0:T(8,128)(2,1)}, bf16[8,48,128]{2,1,0:T(8,128)(2,1)S(1)}, u32[]{:S(2)}) copy-start(bf16[8,48,128]{2,1,0:T(8,128)(2,1)S(1)} %collective-permute-done.r_even) | copy-start | bytes 294916
  9.3 0.6 %copy-start.1 = (bf16[8,48,128]{2,1,0:T(8,128)(2,1)}, bf16[8,48,128]{2,1,0:T(8,128)(2,1)S(1)}, u32[]{:S(2)}) copy-start(bf16[8,48,128]{2,1,0:T(8,128)(2,1)S(1)} %collective-permute-done.1.r_odd) | copy-start | bytes 294916
  12.0 8.6 %collective-permute-start.2 = (bf16[8,72,128]{2,1,0:T(8,128)(2,1)}, bf16[8,72,128]{2,1,0:T(8,128)(2,1)S(1)}, u32[]{:S(2)}, u32[]{:S(2)}) collective-permute-start(bf16[8,72,128]{2,1,0:T(8,128)(2,1)} %get-tuple-element.21), channel_id=1, source_target_pairs={{0,8},{16,24},{32,40},{48,56},{64,72},{80,88},{96,104},{112,120},{... | collective-permute-start | bytes 442376 | tf_op jit(solution)/shard_map/ppermute | solution.py:346
  13.6 8.7 %collective-permute-start.3 = (bf16[8,72,128]{2,1,0:T(8,128)(2,1)}, bf16[8,72,128]{2,1,0:T(8,128)(2,1)S(1)}, u32[]{:S(2)}, u32[]{:S(2)}) collective-permute-start(bf16[8,72,128]{2,1,0:T(8,128)(2,1)} %get-tuple-element.22), channel_id=1, source_target_pairs={{8,16},{24,32},{40,48},{56,64},{72,80},{88,96},{104,112},{120,0},{... | collective-permute-start | bytes 442376 | tf_op jit(solution)/shard_map/ppermute | solution.py:346
  20.6 1.7 %copy-start.2 = (bf16[8,72,128]{2,1,0:T(8,128)(2,1)}, bf16[8,72,128]{2,1,0:T(8,128)(2,1)S(1)}, u32[]{:S(2)}) copy-start(bf16[8,72,128]{2,1,0:T(8,128)(2,1)S(1)} %collective-permute-done.2.x_even) | copy-start | bytes 442372
  22.3 0.7 %copy-start.3 = (bf16[8,72,128]{2,1,0:T(8,128)(2,1)}, bf16[8,72,128]{2,1,0:T(8,128)(2,1)S(1)}, u32[]{:S(2)}) copy-start(bf16[8,72,128]{2,1,0:T(8,128)(2,1)S(1)} %collective-permute-done.3.x_odd) | copy-start | bytes 442372
where the time goes:
time: 38.9 us; the launch traced here: 38.7 us
  Pallas kernels  20.9 us (54%)
  waiting for transfers between devices  7.16 us (18%)
  starting transfers between devices  6.75 us (17%)
  local copies, waits for them, and re-layouts  3.83 us (10%)
    pallas_call x3, Pallas kernels, call(): pl.pallas_call(kernel, out_shape=outs, scratch_shapes=scratch, compiler_p...  20.9 us
    ppermute x4, waiting for transfers between devices, swap(): return lax.ppermute(value, axis, swap_perm(lax.axis_size(axis), odd))  7.16 us
    ppermute x4, starting transfers between devices, swap(): return lax.ppermute(value, axis, swap_perm(lax.axis_size(axis), odd))  6.75 us
    unnamed x9, local copies, waits for them, and re-layouts  3.83 us
  transfers between devices with their start and end apart: 4, of which 3 were waited for; matrix products, arithmetic and copies ran while one was open for 7% of the time, Pallas kernels for 0%

commit v1 on v0

v1 whole, which is shorter than its diff:
```python
import jax
import jax.numpy as jnp
from jax import lax
from jax.experimental import pallas as pl
from jax.experimental.pallas import tpu as pltpu
from jax.sharding import PartitionSpec as P

U = 16
INTERPRET = False
F32 = jnp.float32
BF16 = jnp.bfloat16
N0 = 16
ROW0 = 32
ROWS = 24
SX = 72
SY = 48
FIRST = 8


def far(dx, dy):
    return max(abs(dx), abs(dy)) >= 2 and max(abs(dx), abs(dy)) <= 3


def lanes(c):
    return slice(c * 128, (c + 1) * 128)


def factors(ts, level, dx, dy, c):
    row = (dx + 3) * 7 + dy + 3
    return [ts[row, level : level + 1, lanes(4 * n + c)] for n in range(3)]


def values(ref, c, at):
    return [ref[4 * n + c, at, :] for n in range(3)]


def occupied_rows(cnt_ref, x):
    row = cnt_ref[x : x + 1, :].astype(F32)
    one = lax.broadcasted_iota(jnp.int32, (N0, N0), 0) == lax.broadcasted_iota(jnp.int32, (N0, N0), 1)
    count = jnp.sum(jnp.where(one, jnp.broadcast_to(row, (N0, N0)), 0.0), axis=1, keepdims=True)
    lane = lax.broadcasted_iota(jnp.int32, (N0, 512), 1).astype(F32)
    return lane < count * float(2 * U)


def swap_perm(axis, odd):
    size = (lax.axis_size("row"), lax.axis_size("col"))
    which = ("row", "col").index(axis)
    perm = []
    for row in range(size[0]):
        for col in range(size[1]):
            at = [row, col]
            to = at[which] + (1 if at[which] % 2 == odd else -1)
            if 0 <= to < size[which]:
                at[which] = to
            else:
                at[1 - which] ^= 1
            perm.append((row * size[1] + col, at[0] * size[1] + at[1]))
    return perm


def add_product(acc, factor, value):
    terms = (factor[0] * value[2], factor[1] * value[0], factor[2] * value[1])
    return terms if acc is None else tuple(old + term for old, term in zip(acc, terms))


def complex_sum(acc):
    return acc[0] - acc[2], acc[0] + acc[1]


def opening(out):
    out[...] = jnp.zeros((8, 128), F32)


def upward(first, cur, cnt, rad, shf, msk, f0, p1, p2, p3, m_even, m_odd, c0, me, mo):
    even = (lax.axis_index("col") % 2) == 0
    for x in range(N0):
        kept = jnp.where(occupied_rows(cnt, x), cur[x].astype(F32), 0.0)
        msk[x] = kept.astype(BF16)
        for c in range(4):
            c0[c, x * 16 : (x + 1) * 16, :] = kept[:, lanes(c)]
    lhs = msk[...].reshape(N0 * N0, 512)
    zero = jnp.zeros((8, 128), F32)
    for m in range(2):
        re, im = [
            jnp.dot(lhs, rad[:, n : n + 256], preferred_element_type=F32).astype(BF16).astype(F32)
            for n in (256 * m, 512 + 256 * m)
        ]
        for n, out in enumerate((re, im, re + im)):
            for h in range(2):
                for x in range(N0):
                    base = (x + 2) * ROW0
                    c = 4 * n + 2 * m + h
                    f0[c, base : base + 8, :] = zero
                    f0[c, base + 8 : base + 24, :] = out[x * 16 : (x + 1) * 16, lanes(h)]
                    f0[c, base + 24 : base + 32, :] = zero
    for level, (dest, size) in enumerate(((p1, 8), (p2, 4), (p3, 2))):
        for i in range(size):
            for c in range(4):
                acc = None
                for a in range(2):
                    for b in range(2):
                        if level == 0:
                            at = pl.ds((2 * i + a + 2) * ROW0 + 8 + b, size, stride=2)
                            value = (f0[c, at, :], f0[4 + c, at, :])
                        else:
                            at = pl.ds((2 * i + a) * 8 + b, size, stride=2)
                            value = ((p1, p2)[level - 1][c, at, :], (p1, p2)[level - 1][4 + c, at, :])
                        row = slice(2 * a + b, 2 * a + b + 1)
                        t_re, t_im = shf[level, row, lanes(c)], shf[level, row, lanes(4 + c)]
                        re = t_re * value[0] - t_im * value[1]
                        im = t_re * value[1] + t_im * value[0]
                        acc = (re, im) if acc is None else (acc[0] + re, acc[1] + im)
                dest[c, i * 8 : i * 8 + size, :] = acc[0].astype(BF16).astype(F32)
                dest[4 + c, i * 8 : i * 8 + size, :] = acc[1].astype(BF16).astype(F32)

    def put(c, at, lo, hi):
        me[c, at, :] = jnp.where(even, hi, lo)
        mo[c, at, :] = jnp.where(even, lo, hi)

    for r in range(2):
        for c in range(4):
            lo = c0[c, pl.ds(r, 16, stride=16), :]
            hi = c0[c, pl.ds(14 + r, 16, stride=16), :]
            for h in range(2):
                put(c + 4 * h, pl.ds(r, 8, stride=2), lo[8 * h : 8 * h + 8], hi[8 * h : 8 * h + 8])
        for c in range(8):
            put(c, pl.ds(16 + r, 8, stride=2), p1[c, pl.ds(r, 8, stride=8), :], p1[c, pl.ds(6 + r, 8, stride=8), :])
            put(c, pl.ds(32 + r, 4, stride=2), p2[c, pl.ds(r, 4, stride=8), :], p2[c, pl.ds(2 + r, 4, stride=8), :])
            both = p3[c, pl.ds(r, 2, stride=8), :]
            put(c, pl.ds(40 + r, 2, stride=2), both, both)
    for c in range(8):
        me[c, 44:48, :] = jnp.zeros((4, 128), F32)
        mo[c, 44:48, :] = jnp.zeros((4, 128), F32)
        m_even[c] = me[c].astype(BF16)
        m_odd[c] = mo[c].astype(BF16)


def leaf(f0, ts, inc, i):
    for c in range(4):
        acc = {}
        for xs in range(6):
            if not 0 <= 2 * i + xs - 2 < N0:
                continue
            for k in range(6):
                if xs in (2, 3) and k in (2, 3):
                    continue
                value = values(f0, c, pl.ds((2 * i + xs) * ROW0 + 6 + k, 8, stride=2))
                for a in range(2):
                    for b in range(2):
                        dx, dy = xs - 2 - a, k - 2 - b
                        if far(dx, dy):
                            acc[a, b] = add_product(acc.get((a, b)), factors(ts, 0, dx, dy, c), value)
        for (a, b), sums in acc.items():
            for q, total in enumerate(complex_sum(sums)):
                inc[4 * q + c, pl.ds((2 * i + a) * 16 + b, 8, stride=2), :] = total


def inside(f0, tr, inc, ts):
    re, im = tr[:, :, 0:512], tr[:, :, 512:1024]
    ts[:, :, 0:512] = re
    ts[:, :, 512:1024] = im - re
    ts[:, :, 1024:1536] = re + im
    for i in range(FIRST):
        leaf(f0, ts, inc, i)


def received(axis, r_even, r_odd, lo, hi):
    me = lax.axis_index(axis)
    last = lax.axis_size(axis) - 1
    even = (me % 2) == 0
    for c in range(8):
        from_even = r_even[c].astype(F32)
        from_odd = r_odd[c].astype(F32)
        lo[c] = jnp.where(me == 0, 0.0, jnp.where(even, from_odd, from_even))
        hi[c] = jnp.where(me == last, 0.0, jnp.where(even, from_even, from_odd))


def strips(r_even, r_odd, msk, p1, p2, p3, x_even, x_odd, ylo, yhi, mlo, mhi):
    received("col", r_even, r_odd, ylo, yhi)
    even = (lax.axis_index("row") % 2) == 0
    for dest, first in ((mlo, 0), (mhi, 1)):
        for xr in range(2):
            x = 14 * first + xr
            kept = msk[x].astype(F32)
            for c in range(4):
                dest[4 * xr + c, 2:18, :] = kept[:, lanes(c)]
                at = slice(2 * (x % 8), 2 * (x % 8) + 2)
                dest[4 * xr + c, 0:2, :] = ylo[c + 4 * (x // 8), at, :]
                dest[4 * xr + c, 18:20, :] = yhi[c + 4 * (x // 8), at, :]
            for c in range(8):
                for level_ref, size, base, within in ((p1, 8, 32, 16), (p2, 4, 56, 32), (p3, 2, 20, 40)):
                    x = (size - 2) * first + xr
                    at = base + (size + 4) * xr
                    dest[c, at + 2 : at + 2 + size, :] = level_ref[c, x * 8 : x * 8 + size, :]
                    dest[c, at : at + 2, :] = ylo[c, within + 2 * x : within + 2 * x + 2, :]
                    dest[c, at + 2 + size : at + 4 + size, :] = yhi[c, within + 2 * x : within + 2 * x + 2, :]
    for c in range(8):
        lo = mlo[c]
        hi = mhi[c]
        x_even[c] = jnp.where(even, hi, lo).astype(BF16)
        x_odd[c] = jnp.where(even, lo, hi).astype(BF16)


def beside_y(
    r_even, r_odd, msk, f0, p1, p2, p3, inc0, rad, near, tr, ts, base0, near_base, t_rr, t_ii, own1, own2, own3,
    ylo, yhi, hy, hc, f1, g1, box, swapped, out, cx, ln,
):
    received("col", r_even, r_odd, ylo, yhi)
    blocks = []
    zero = jnp.zeros((8, 128), F32)
    for s, src in enumerate((ylo, yhi)):
        for r in range(2):
            both = [
                jnp.concatenate([src[4 * h + c, pl.ds(r, 8, stride=2), :] for c in range(4)], axis=1) for h in range(2)
            ]
            blocks.append(jnp.concatenate(both, axis=0))
        touching = blocks[2 * s + 1 - s]
        for c in range(4):
            hc[s, c, 0:8, :] = zero
            hc[s, c, 8:24, :] = touching[:, lanes(c)]
            hc[s, c, 24:32, :] = zero
    halo = jnp.dot(jnp.concatenate(blocks, axis=0).astype(BF16), rad[...], preferred_element_type=F32)
    halo = halo.astype(BF16).astype(F32)
    for c in range(4):
        re, im = halo[:, lanes(c)], halo[:, lanes(4 + c)]
        for q, part in enumerate((re, im, re + im)):
            for n in range(4):
                hy[4 * q + c, n * 32 : n * 32 + 8, :] = zero
                hy[4 * q + c, n * 32 + 8 : n * 32 + 24, :] = part[16 * n : 16 * n + 16]
                hy[4 * q + c, n * 32 + 24 : n * 32 + 32, :] = zero
    for dx in range(-3, 4):
        for dy in range(-3, 4):
            if far(dx, dy):
                row = (dx + 3) * 7 + dy + 3
                for c in range(4):
                    re = tr[row, 2:4, lanes(c)]
                    im = tr[row, 2:4, lanes(4 + c)]
                    t_rr[pl.ds(row * 8 + c, 2, stride=392), :] = re
                    t_rr[pl.ds(row * 8 + 4 + c, 2, stride=392), :] = re
                    t_ii[pl.ds(row * 8 + c, 2, stride=392), :] = -im
                    t_ii[pl.ds(row * 8 + 4 + c, 2, stride=392), :] = im
    for c in range(8):
        base0[c, 0 : FIRST * 32, :] = inc0[c]
    for i in range(FIRST, 8):
        leaf(f0, ts, base0, i)
    for x in range(N0):
        kept = msk[x].astype(F32)
        for c in range(4):
            cx[c, x * ROW0 : x * ROW0 + 8, :] = zero
            cx[c, x * ROW0 + 8 : x * ROW0 + 24, :] = kept[:, lanes(c)]
            cx[c, x * ROW0 + 24 : x * ROW0 + 32, :] = zero
    ln[0] = jnp.zeros((16, 1536), BF16)
    ln[17] = jnp.zeros((16, 1536), BF16)
    for dy in range(3):
        for x in range(N0):
            for c in range(4):
                at = x * ROW0 + 7 + dy
                ln[x + 1, :, lanes(4 * dy + c)] = cx[c, at : at + 16, :].astype(BF16)
    total = None
    for dx in range(3):
        rows = ln[dx : dx + 16].reshape(N0 * N0, 1536)
        term = jnp.dot(rows, near[3 * dx : 3 * dx + 3].reshape(1536, 512), preferred_element_type=F32)
        total = term if total is None else total + term
    for c in range(4):
        near_base[c] = total[:, lanes(c)]
    for s in range(2):
        for c in range(4):
            acc = {}
            for r in range(2):
                for xs in range(6):
                    value = values(hy, c, pl.ds((2 * s + r) * 32 + 6 + xs, 8, stride=2))
                    for a in range(2):
                        for b in range(2):
                            dx, dy = xs - 2 - a, 4 * s - 2 + r - b
                            if far(dx, dy):
                                acc[a, b] = add_product(acc.get((a, b)), factors(ts, 0, dx, dy, c), value)
            for (a, b), sums in acc.items():
                for q, total in enumerate(complex_sum(sums)):
                    at = pl.ds(16 * a + 14 * s + b, 8, stride=32)
                    base0[4 * q + c, at, :] = base0[4 * q + c, at, :] + total
        total = None
        for dx in range(3):
            rows = jnp.concatenate([hc[s, c, 7 + dx : 23 + dx, :] for c in range(4)], axis=1).astype(BF16)
            term = jnp.dot(rows, near[3 * dx + 2 * s], preferred_element_type=F32)
            total = term if total is None else total + term
        for c in range(4):
            at = pl.ds(15 * s, 16, stride=16)
            near_base[c, at, :] = near_base[c, at, :] + total[:, lanes(c)]
    for level, size, own, base, inc in ((3, 2, p3, 40, own3), (2, 4, p2, 32, own2)):
        rows = [
            (x + 2, [(2, size, own, x * 8), (0, 2, ylo, base + 2 * x), (size + 2, 2, yhi, base + 2 * x)])
            for x in range(size)
        ]
        by_box(level, size, rows, t_rr, t_ii, box, swapped, out)
        for c in range(8):
            for x in range(size):
                inc[c, x * 8 : x * 8 + size, :] = out[pl.ds(x * size * 8 + c, size, stride=8), :]
    for c in range(8):
        for x in range(8):
            base = x * ROWS
            f1[c, base + 8 : base + 16, :] = p1[c, x * 8 : x * 8 + 8, :]
            f1[c, base + 6 : base + 8, :] = ylo[c, 16 + 2 * x : 18 + 2 * x, :]
            f1[c, base + 16 : base + 18, :] = yhi[c, 16 + 2 * x : 18 + 2 * x, :]
    for c in range(4):
        for s in range(3):
            for xe in range(8):
                for h in range(2):
                    x = xe + 4 * h - 2
                    at = slice(xe * 16 + 8 * h, xe * 16 + 8 * h + 8)
                    if 0 <= x < 8:
                        base = x * ROWS + 6 + 2 * s
                        re, im = f1[c, base : base + 8, :], f1[4 + c, base : base + 8, :]
                        parts = (re, im, re + im)
                    else:
                        parts = (zero, zero, zero)
                    for q, part in enumerate(parts):
                        g1[s, 4 * q + c, at, :] = part
    for i in range(2):
        for c in range(4):
            acc = {}
            for xs in range(6):
                for k in range(6):
                    if xs in (2, 3) and k in (2, 3):
                        continue
                    at = pl.ds((2 * i + xs) * 16 + k % 2, 8, stride=2)
                    value = [g1[k // 2, 4 * q + c, at, :] for q in range(3)]
                    for a in range(2):
                        for b in range(2):
                            dx, dy = xs - 2 - a, k - 2 - b
                            if far(dx, dy):
                                acc[a, b] = add_product(acc.get((a, b)), factors(ts, 1, dx, dy, c), value)
            for (a, b), sums in acc.items():
                for q, total in enumerate(complex_sum(sums)):
                    for h in range(2):
                        at = pl.ds((2 * (i + 2 * h) + a) * 8 + b, 4, stride=2)
                        own1[4 * q + c, at, :] = total[4 * h : 4 * h + 4]


def add_parent(inc, parent, shf, level, size):
    half = size // 2
    for x in range(size):
        for b in range(2):
            row = slice(2 * (x % 2) + b, 2 * (x % 2) + b + 1)
            at = pl.ds(x * 8 + b, half, stride=2)
            for c in range(4):
                q_re = parent[c, (x // 2) * 8 : (x // 2) * 8 + half, :]
                q_im = parent[4 + c, (x // 2) * 8 : (x // 2) * 8 + half, :]
                t_re = shf[level, row, lanes(c)]
                t_im = shf[level, row, lanes(4 + c)]
                inc[c, at, :] = inc[c, at, :] + (t_re * q_re + t_im * q_im)
                inc[4 + c, at, :] = inc[4 + c, at, :] + (t_re * q_im - t_im * q_re)


def by_box(level, size, rows, t_rr, t_ii, box, swapped, out):
    wide = size + 4
    for c in range(8):
        for xe, pieces in rows:
            for ye, count, src, at in pieces:
                piece = src[c, at : at + count, :]
                first = (xe * wide + ye) * 8
                box[pl.ds(first + c, count, stride=8), :] = piece
                swapped[pl.ds(first + (c + 4) % 8, count, stride=8), :] = piece
    given = [xe for xe, _ in rows]
    for i in range(size // 2):
        for j in range(size // 2):
            acc = {}
            for xs in range(6):
                if 2 * i + xs not in given:
                    continue
                for k in range(6):
                    if xs in (2, 3) and k in (2, 3):
                        continue
                    at = ((2 * i + xs) * wide + 2 * j + k) * 8
                    value = box[at : at + 8, :]
                    other = swapped[at : at + 8, :]
                    for a in range(2):
                        for b in range(2):
                            dx, dy = xs - 2 - a, k - 2 - b
                            if far(dx, dy):
                                row = (level - 2) * 392 + ((dx + 3) * 7 + dy + 3) * 8
                                term = t_rr[row : row + 8, :] * value + t_ii[row : row + 8, :] * other
                                acc[a, b] = term if (a, b) not in acc else acc[a, b] + term
            for a in range(2):
                for b in range(2):
                    at = ((2 * i + a) * size + 2 * j + b) * 8
                    out[at : at + 8, :] = acc.get((a, b), jnp.zeros((8, 128), F32))


def downward(
    cnt, inc0, near_base, t_rr, t_ii, own1, own2, own3, x_even, x_odd, rad, rec, near, ts, shf,
    field, xlo, xhi, hc, hx, xs1, box, swapped, out, tot, inc1, inc2, inc3, half,
):
    received("row", x_even, x_odd, xlo, xhi)
    sides = []
    for s, src in enumerate((xlo, xhi)):
        for xr in range(2):
            sides.append(jnp.concatenate([src[4 * xr + c, 0:32, :] for c in range(4)], axis=1))
        for c in range(4):
            hc[s, c, 0:24, :] = src[4 * (1 - s) + c, 0:24, :]
    halo = jnp.dot(jnp.concatenate(sides, axis=0).astype(BF16), rad[...], preferred_element_type=F32)
    halo = halo.astype(BF16).astype(F32)
    for c in range(4):
        re, im = halo[:, lanes(c)], halo[:, lanes(4 + c)]
        for q, part in enumerate((re, im, re + im)):
            hx[4 * q + c] = part
        for s, src in enumerate((xlo, xhi)):
            re, im = src[c, 32:56, :], src[4 + c, 32:56, :]
            for q, part in enumerate((re, im, re + im)):
                xs1[4 * q + c, s * 24 : s * 24 + 24, :] = part

    for level, size, base, own, inc in ((3, 2, 20, own3, inc3), (2, 4, 56, own2, inc2)):
        wide = size + 4
        rows = [
            (xe + xr, [(0, wide, src, base + wide * xr)]) for src, xe in ((xlo, 0), (xhi, size + 2)) for xr in range(2)
        ]
        by_box(level, size, rows, t_rr, t_ii, box, swapped, out)
        for c in range(8):
            for x in range(size):
                at = slice(x * 8, x * 8 + size)
                inc[c, at, :] = own[c, at, :] + out[pl.ds(x * size * 8 + c, size, stride=8), :]
    add_parent(inc2, inc3, shf, 2, 4)
    for c in range(8):
        inc1[c] = own1[c]
    for s in range(2):
        for c in range(4):
            acc = {}
            for xr in range(2):
                xs = 4 * s + xr
                for k in range(6):
                    value = values(xs1, c, pl.ds((2 * s + xr) * 12 + k, 4, stride=2))
                    for a in range(2):
                        for b in range(2):
                            dx, dy = xs - 2 - a, k - 2 - b
                            if far(dx, dy):
                                acc[a, b] = add_product(acc.get((a, b)), factors(ts, 1, dx, dy, c), value)
            for (a, b), sums in acc.items():
                at = pl.ds((6 * s + a) * 8 + b, 4, stride=2)
                for q, total in enumerate(complex_sum(sums)):
                    inc1[4 * q + c, at, :] = inc1[4 * q + c, at, :] + total
    add_parent(inc1, inc2, shf, 1, 8)

    for x in range(N0):
        for b in range(2):
            row = slice(2 * (x % 2) + b, 2 * (x % 2) + b + 1)
            at = pl.ds(x * 16 + b, 8, stride=2)
            for c in range(4):
                q_re = inc1[c, (x // 2) * 8 : (x // 2) * 8 + 8, :]
                q_im = inc1[4 + c, (x // 2) * 8 : (x // 2) * 8 + 8, :]
                t_re = shf[0, row, lanes(c)]
                t_im = shf[0, row, lanes(4 + c)]
                tot[c, at, :] = inc0[c, at, :] + (t_re * q_re + t_im * q_im)
                tot[4 + c, at, :] = inc0[4 + c, at, :] + (t_re * q_im - t_im * q_re)
    for s in range(2):
        for c in range(4):
            acc = {}
            for xr in range(2):
                xs = 4 * s + xr
                for k in range(6):
                    value = values(hx, c, pl.ds((2 * s + xr) * 32 + k, 8, stride=2))
                    for a in range(2):
                        for b in range(2):
                            dx, dy = xs - 2 - a, k - 2 - b
                            if far(dx, dy):
                                acc[a, b] = add_product(acc.get((a, b)), factors(ts, 0, dx, dy, c), value)
            for (a, b), sums in acc.items():
                at = pl.ds((14 * s + a) * 16 + b, 8, stride=2)
                for q, total in enumerate(complex_sum(sums)):
                    tot[4 * q + c, at, :] = tot[4 * q + c, at, :] + total
    for c in range(8):
        half[:, lanes(c)] = tot[c].astype(BF16)
    side = []
    for s in range(2):
        total = None
        for dy in range(3):
            rows = jnp.concatenate([hc[s, c, 1 + dy : 17 + dy, :] for c in range(4)], axis=1).astype(BF16)
            term = jnp.dot(rows, near[6 * s + dy], preferred_element_type=F32)
            total = term if total is None else total + term
        side.append(total)
    total = jnp.dot(half[...], rec[...], preferred_element_type=F32)
    for x in range(N0):
        here = slice(x * 16, (x + 1) * 16)
        result = total[here] + jnp.concatenate([near_base[c, here, :] for c in range(4)], axis=1)
        if x in (0, N0 - 1):
            result = result + side[x // (N0 - 1)]
        field[x] = jnp.where(occupied_rows(cnt, x), result, 0.0).astype(BF16)


def call(kernel, outs, scratch, flops, *args):
    place = pl.BlockSpec(memory_space=pltpu.VMEM)
    return pl.pallas_call(
        kernel,
        out_shape=outs,
        in_specs=[place] * len(args),
        out_specs=[place] * len(outs),
        scratch_shapes=scratch,
        compiler_params=pltpu.CompilerParams(vmem_limit_bytes=16 * 1024 * 1024),
        cost_estimate=pl.CostEstimate(flops=flops, bytes_accessed=1 << 20, transcendentals=0),
        interpret=INTERPRET,
    )(*args)


def shape(dims, kind):
    return jax.ShapeDtypeStruct(dims, kind)


def swap(value, axis, odd):
    return lax.ppermute(value, ("row", "col"), swap_perm(axis, odd))


def shards(currents, counts, radiate, receive, near_blocks, translate, shift):
    mem = pltpu.VMEM
    factor = jnp.transpose(translate, (1, 0, 2))
    ys, xs = mem((8, SY, 128), F32), mem((8, SX, 128), F32)
    (first,) = call(opening, [shape((8, 128), F32)], [], 10**13)
    masked, f0, p1, p2, p3, m_even, m_odd = call(
        upward,
        [
            shape((16, 16, 512), BF16),
            shape((12, 20 * ROW0, 128), F32),
            shape((8, 64, 128), F32),
            shape((8, 32, 128), F32),
            shape((8, 16, 128), F32),
            shape((8, SY, 128), BF16),
            shape((8, SY, 128), BF16),
        ],
        [mem((4, 256, 128), F32), ys, ys],
        10**12,
        first, currents, counts, radiate, shift,
    )
    r_even = swap(m_even, "col", 0)
    r_odd = swap(m_odd, "col", 1)
    inc0, sums = call(
        inside,
        [shape((8, 32 * FIRST, 128), F32), shape((49, 4, 1536), F32)],
        [],
        4 * 10**9,
        f0, factor,
    )
    r_even, r_odd, inc0 = lax.optimization_barrier((r_even, r_odd, inc0))
    s_even, s_odd = call(
        strips,
        [shape((8, SX, 128), BF16)] * 2,
        [ys, ys, xs, xs],
        10**7,
        r_even, r_odd, masked, p1, p2, p3,
    )
    x_even = swap(s_even, "row", 0)
    x_odd = swap(s_odd, "row", 1)
    inc0, near_sum, t_rr, t_ii, own1, own2, own3 = call(
        beside_y,
        [
            shape((8, 256, 128), F32), shape((4, 256, 128), F32), shape((784, 128), F32), shape((784, 128), F32),
            shape((8, 64, 128), F32), shape((8, 32, 128), F32), shape((8, 16, 128), F32),
        ],
        [
            ys, ys, mem((12, 128, 128), F32), mem((2, 4, 32, 128), F32), mem((8, 8 * ROWS, 128), F32),
            mem((3, 12, 128, 128), F32), mem((512, 128), F32), mem((512, 128), F32), mem((128, 128), F32),
            mem((4, 16 * ROW0, 128), F32), mem((18, 16, 1536), BF16),
        ],
        10**9,
        r_even, r_odd, masked, f0, p1, p2, p3, inc0, radiate, near_blocks, factor, sums,
    )
    (field,) = call(
        downward,
        [shape((16, 16, 512), BF16)],
        [
            xs, xs, mem((2, 4, 24, 128), F32), mem((12, 128, 128), F32), mem((12, 48, 128), F32),
            mem((512, 128), F32), mem((512, 128), F32), mem((128, 128), F32),
            mem((8, 256, 128), F32), mem((8, 64, 128), F32), mem((8, 32, 128), F32), mem((8, 16, 128), F32),
            mem((256, 1024), BF16),
        ],
        3 * 10**9,
        counts, inc0, near_sum, t_rr, t_ii, own1, own2, own3, x_even, x_odd,
        radiate, receive, near_blocks, sums, shift,
    )
    return field


def solution(mesh):
    return jax.shard_map(
        shards,
        mesh=mesh,
        in_specs=(P("row", "col", None), P("row", "col"), P(), P(), P(), P(), P()),
        out_specs=P("row", "col", None),
        check_vma=False,
    )
```

time: 38.9 us -> 19.9 us (0.51)
  the two profiles are of different devices: /device:TPU:25 before, /device:TPU:6 now
where the time goes in v1:
time: 19.9 us; the launch traced here: 19.8 us
  Pallas kernels  11 us (55%)
  starting transfers between devices  6.71 us (34%)
  local copies, waits for them, and re-layouts  1.29 us (6%)
  waiting for transfers between devices  0.72 us (4%)
    pallas_call x6, Pallas kernels, call(): pl.pallas_call(kernel, out_shape=outs, in_specs=[place] * len(args), out_...  11 us
    ppermute x4, starting transfers between devices, swap(): return lax.ppermute(value, ('row', 'col'), swap_perm(axis, odd))  6.71 us
    unnamed x16, local copies, waits for them, and re-layouts  1.29 us
    ppermute x4, waiting for transfers between devices, swap(): return lax.ppermute(value, ('row', 'col'), swap_perm(axis, odd))  0.72 us
  transfers between devices with their start and end apart: 4, of which 1 were waited for; matrix products, arithmetic and copies ran while one was open for 0% of the time, Pallas kernels for 35%

profile of v1, /device:TPU:6, one launch (start us, length us, event | category | flops | bytes accessed | tf_op | source)
XLA Modules:
  0.0 19.8 jit_solution(7919520448950569905)
XLA Ops:
  0.0 0.0 copy-start
  0.0 0.0 copy-start.3
  0.0 0.0 copy-start.4
  0.0 0.0 copy-start.5
  0.0 1.2 %copy-done = bf16[512,1024]{1,0:T(8,128)(2,1)S(1)} copy-done((bf16[512,1024]{1,0:T(8,128)(2,1)S(1)}, bf16[512,1024]{1,0:T(8,128)(2,1)}, u32[]{:S(2)}) %copy-start) | copy-done | bytes 1048600
  1.2 0.0 copy-done.3
  1.2 0.0 copy-done.4
  1.2 0.1 copy-done.5
  1.3 0.0 copy-start.2
  1.3 1.0 %shard_map.74 = (bf16[16,16,512]{2,1,0:T(8,128)(2,1)S(1)}, f32[12,640,128]{2,1,0:T(8,128)S(1)}, f32[8,64,128]{2,1,0:T(8,128)S(1)}, f32[8,32,128]{2,1,0:T(8,128)S...) custom-call(f32[8,128]{1,0:T(8,128)S(1)} %shard_map.73.first, ...), custom_call_target="tpu_custom_call" | custom-call | flops 999999995904 | bytes 1048576 | tf_op jit(solution)/shard_map/pallas_call | solution.py:490
  2.3 0.1 collective-permute-start
  2.4 2.0 %collective-permute-start.1 = (bf16[8,48,128]{2,1,0:T(8,128)(2,1)S(1)}, bf16[8,48,128]{2,1,0:T(8,128)(2,1)S(1)}, u32[]{:S(2)}, u32[]{:S(2)}) collective-permute-start(bf16[8,48,128]{2,1,0:T(8,128)(2,1)S(1)} %get-tuple-element.27), channel_id=1, source_target_pairs={{0,8},{1,2},{2,1},{3,4},{4,3},{5,6},{6,5},{7,15},{8,0},{9,10},{10,... | collective-permute-start | bytes 294920 | tf_op jit(solution)/shard_map/ppermute | solution.py:507
  4.4 0.0 slice-start
  4.4 0.0 copy-done.2
  4.4 0.0 slice-start.1
  4.4 2.8 %shard_map.75 = (f32[8,256,128]{2,1,0:T(8,128)S(1)}, f32[49,4,1536]{2,1,0:T(4,128)S(1)}) custom-call(f32[12,640,128]{2,1,0:T(8,128)S(1)} %get-tuple-element.28.f0, f32[49,4,1024]{2,1,0:T(4,128)S(1)} %bitcast.3), custom_call_target="tpu_custom_call" | custom-call | flops 4000000000 | bytes 1048576 | tf_op jit(solution)/shard_map/pallas_call | solution.py:490
  7.2 0.0 collective-permute-done.r_even
  7.2 0.0 collective-permute-done.1.r_odd
  7.2 0.2 shard_map.77
  7.4 1.8 %collective-permute-start.2 = (bf16[8,72,128]{2,1,0:T(8,128)(2,1)S(1)}, bf16[8,72,128]{2,1,0:T(8,128)(2,1)S(1)}, u32[]{:S(2)}, u32[]{:S(2)}) collective-permute-start(bf16[8,72,128]{2,1,0:T(8,128)(2,1)S(1)} %get-tuple-element.45), channel_id=1, source_target_pairs={{0,8},{1,9},{2,10},{3,11},{4,12},{5,13},{6,14},{7,15},{8,0},{9,1},... | collective-permute-start | bytes 442376 | tf_op jit(solution)/shard_map/ppermute | solution.py:507
  9.2 2.8 %collective-permute-start.3 = (bf16[8,72,128]{2,1,0:T(8,128)(2,1)S(1)}, bf16[8,72,128]{2,1,0:T(8,128)(2,1)S(1)}, u32[]{:S(2)}, u32[]{:S(2)}) collective-permute-start(bf16[8,72,128]{2,1,0:T(8,128)(2,1)S(1)} %get-tuple-element.46), channel_id=1, source_target_pairs={{0,1},{1,0},{2,3},{3,2},{4,5},{5,4},{6,7},{7,6},{8,16},{9,17},{10,... | collective-permute-start | bytes 442376 | tf_op jit(solution)/shard_map/ppermute | solution.py:507
  12.0 0.0 slice-done
  12.0 0.0 slice-done.1
  12.0 0.0 copy-start.1
  12.0 4.2 %shard_map.76 = (f32[8,256,128]{2,1,0:T(8,128)S(1)}, f32[4,256,128]{2,1,0:T(8,128)S(1)}, f32[784,128]{1,0:T(8,128)S(1)}, f32[784,128]{1,0:T(8,128)S(1)}, f32[8,6...) custom-call(bf16[8,48,128]{2,1,0:T(8,128)(2,1)S(1)} %collective-permute-done.r_even, ...), custom_call_target="tpu_custom_call" | custom-call | flops 1000000000 | bytes 1048576 | tf_op jit(solution)/shard_map/pallas_call | solution.py:490
  16.2 0.0 collective-permute-done.2.x_even
  16.2 0.7 %collective-permute-done.3.x_odd = bf16[8,72,128]{2,1,0:T(8,128)(2,1)S(1)} collective-permute-done((bf16[8,72,128]{2,1,0:T(8,128)(2,1)S(1)}, bf16[8,72,128]{2,1,0:T(8,128)(2,1)S(1)}, u32[]{:S(2)}, u32[]{:S(2)}) %collective-permute-start.3) | collective-permute-done | bytes 147488 | tf_op jit(solution)/shard_map/ppermute | solution.py:507
  16.9 0.0 copy-done.1
  16.9 2.8 %shard_map.78 = bf16[16,16,512]{2,1,0:T(8,128)(2,1)} custom-call(s32[16,16]{1,0:T(8,128)S(1)} %copy-done.4, f32[8,256,128]{2,1,0:T(8,128)S(1)} %get-tuple-element.38.inc0, f32[4,256,128]{2,1,0:T(8,128)S(1)} %get-tuple-element.39.near_base, f32[784,128]{1,0:T(8,128)S(1)} %get-tuple-element.40.t_rr, f32[784,128]{1,0:T(8,128)S(1)} %get-tuple-element.41.t_ii, ...), custom_call_target="tpu_custom_call" | custom-call | flops 3000000000 | bytes 1048576 | tf_op jit(solution)/shard_map/pallas_call | solution.py:490
  (2 shorter events, 0.0 us)
Async XLA Ops:
  0.0 1.2 %copy-start = (bf16[512,1024]{1,0:T(8,128)(2,1)S(1)}, bf16[512,1024]{1,0:T(8,128)(2,1)}, u32[]{:S(2)}) copy-start(bf16[512,1024]{1,0:T(8,128)(2,1)} %rad.5) | copy-start | bytes 3145732
  0.0 1.2 %copy-start.3 = (f32[3,4,1024]{2,1,0:T(4,128)S(1)}, f32[3,4,1024]{2,1,0:T(4,128)}, u32[]{:S(2)}) copy-start(f32[3,4,1024]{2,1,0:T(4,128)} %shf.3) | copy-start | bytes 147460
  0.0 1.2 %copy-start.4 = (s32[16,16]{1,0:T(8,128)S(1)}, s32[16,16]{1,0:T(8,128)}, u32[]{:S(2)}) copy-start(s32[16,16]{1,0:T(8,128)} %cnt.3) | copy-start | bytes 3076
  0.0 1.3 %copy-start.5 = (bf16[16,16,512]{2,1,0:T(8,128)(2,1)S(1)}, bf16[16,16,512]{2,1,0:T(8,128)(2,1)}, u32[]{:S(2)}) copy-start(bf16[16,16,512]{2,1,0:T(8,128)(2,1)} %cur.1) | copy-start | bytes 786436
  1.3 3.1 %copy-start.2 = (f32[4,49,1024]{2,0,1:T(4,128)S(1)}, f32[4,49,1024]{2,0,1:T(4,128)}, u32[]{:S(2)}) copy-start(f32[4,49,1024]{2,0,1:T(4,128)} %param.12) | copy-start | bytes 2408452
  2.3 4.9 %collective-permute-start = (bf16[8,48,128]{2,1,0:T(8,128)(2,1)S(1)}, bf16[8,48,128]{2,1,0:T(8,128)(2,1)S(1)}, u32[]{:S(2)}, u32[]{:S(2)}) collective-permute-start(bf16[8,48,128]{2,1,0:T(8,128)(2,1)S(1)} %get-tuple-element.26), channel_id=1, source_target_pairs={{0,1},{1,0},{2,3},{3,2},{4,5},{5,4},{6,7},{7,6},{8,9},{9,8},{10,11... | collective-permute-start | bytes 294920 | tf_op jit(solution)/shard_map/ppermute | solution.py:507
  2.4 4.8 %collective-permute-start.1 = (bf16[8,48,128]{2,1,0:T(8,128)(2,1)S(1)}, bf16[8,48,128]{2,1,0:T(8,128)(2,1)S(1)}, u32[]{:S(2)}, u32[]{:S(2)}) collective-permute-start(bf16[8,48,128]{2,1,0:T(8,128)(2,1)S(1)} %get-tuple-element.27), channel_id=1, source_target_pairs={{0,8},{1,2},{2,1},{3,4},{4,3},{5,6},{6,5},{7,15},{8,0},{9,10},{10,... | collective-permute-start | bytes 294920 | tf_op jit(solution)/shard_map/ppermute | solution.py:507
  4.4 7.7 %slice-start = ((s8[4718592]{0:T(1024)(128)(4,1)}), s8[4194304]{0:T(1024)(128)(4,1)S(1)}, s32[]{:S(2)}) async-start(s8[4718592]{0:T(1024)(128)(4,1)} %bitcast.1), calls=%async_computation | async-start | bytes 8388608
  4.4 7.7 %slice-start.1 = ((s8[4718592]{0:T(1024)(128)(4,1)}), s8[524288]{0:T(1024)(128)(4,1)S(1)}, s32[]{:S(2)}) async-start(s8[4718592]{0:T(1024)(128)(4,1)} %bitcast.1), calls=%async_computation.1 | async-start | bytes 1048576
  7.4 8.8 %collective-permute-start.2 = (bf16[8,72,128]{2,1,0:T(8,128)(2,1)S(1)}, bf16[8,72,128]{2,1,0:T(8,128)(2,1)S(1)}, u32[]{:S(2)}, u32[]{:S(2)}) collective-permute-start(bf16[8,72,128]{2,1,0:T(8,128)(2,1)S(1)} %get-tuple-element.45), channel_id=1, source_target_pairs={{0,8},{1,9},{2,10},{3,11},{4,12},{5,13},{6,14},{7,15},{8,0},{9,1},... | collective-permute-start | bytes 442376 | tf_op jit(solution)/shard_map/ppermute | solution.py:507
  9.2 7.7 %collective-permute-start.3 = (bf16[8,72,128]{2,1,0:T(8,128)(2,1)S(1)}, bf16[8,72,128]{2,1,0:T(8,128)(2,1)S(1)}, u32[]{:S(2)}, u32[]{:S(2)}) collective-permute-start(bf16[8,72,128]{2,1,0:T(8,128)(2,1)S(1)} %get-tuple-element.46), channel_id=1, source_target_pairs={{0,1},{1,0},{2,3},{3,2},{4,5},{5,4},{6,7},{7,6},{8,16},{9,17},{10,... | collective-permute-start | bytes 442376 | tf_op jit(solution)/shard_map/ppermute | solution.py:507
  12.0 4.9 %copy-start.1 = (bf16[1024,512]{1,0:T(8,128)(2,1)S(1)}, bf16[1024,512]{1,0:T(8,128)(2,1)}, u32[]{:S(2)}) copy-start(bf16[1024,512]{1,0:T(8,128)(2,1)} %rec.1) | copy-start | bytes 3145732

commit v2 on v1

--- a/solution.py
+++ b/solution.py
@@ -13,8 +13,9 @@
 ROW0 = 32
 ROWS = 24
 SX = 72
+MX = 48
 SY = 48
-FIRST = 8
+FIRST = 7
 
 
 def far(dx, dy):
@@ -34,11 +35,14 @@
     return [ref[4 * n + c, at, :] for n in range(3)]
 
 
-def occupied_rows(cnt_ref, x):
+def count_rows(cnt_ref, x):
     row = cnt_ref[x : x + 1, :].astype(F32)
     one = lax.broadcasted_iota(jnp.int32, (N0, N0), 0) == lax.broadcasted_iota(jnp.int32, (N0, N0), 1)
-    count = jnp.sum(jnp.where(one, jnp.broadcast_to(row, (N0, N0)), 0.0), axis=1, keepdims=True)
-    lane = lax.broadcasted_iota(jnp.int32, (N0, 512), 1).astype(F32)
+    return jnp.sum(jnp.where(one, jnp.broadcast_to(row, (N0, N0)), 0.0), axis=1, keepdims=True)
+
+
+def occupied(count, c):
+    lane = lax.broadcasted_iota(jnp.int32, count.shape, 1).astype(F32) + float(128 * c)
     return lane < count * float(2 * U)
 
 
@@ -67,19 +71,28 @@
     return acc[0] - acc[2], acc[0] + acc[1]
 
 
-def opening(out):
-    out[...] = jnp.zeros((8, 128), F32)
-
-
-def upward(first, cur, cnt, rad, shf, msk, f0, p1, p2, p3, m_even, m_odd, c0, me, mo):
+def opening(f0):
+    zero = jnp.zeros((8, 128), F32)
+    for c in range(12):
+        for x in range(N0):
+            base = (x + 2) * ROW0
+            f0[c, base : base + 8, :] = zero
+            f0[c, base + 24 : base + 32, :] = zero
+
+
+def mask(cur, cnt, msk, c0, count):
+    for x in range(N0):
+        here = slice(x * 16, (x + 1) * 16)
+        count[here, :] = jnp.broadcast_to(count_rows(cnt, x), (N0, 128))
+        for c in range(4):
+            kept = jnp.where(occupied(count[here, :], c), cur[x, :, lanes(c)].astype(F32), 0.0)
+            msk[x, :, lanes(c)] = kept.astype(BF16)
+            c0[c, here, :] = kept
+
+
+def upward(f0_zero, msk, c0, rad, shf, f0, p1, p2, p3, m_odd, m_even, me, mo):
     even = (lax.axis_index("col") % 2) == 0
-    for x in range(N0):
-        kept = jnp.where(occupied_rows(cnt, x), cur[x].astype(F32), 0.0)
-        msk[x] = kept.astype(BF16)
-        for c in range(4):
-            c0[c, x * 16 : (x + 1) * 16, :] = kept[:, lanes(c)]
     lhs = msk[...].reshape(N0 * N0, 512)
-    zero = jnp.zeros((8, 128), F32)
     for m in range(2):
         re, im = [
             jnp.dot(lhs, rad[:, n : n + 256], preferred_element_type=F32).astype(BF16).astype(F32)
@@ -90,9 +103,7 @@
                 for x in range(N0):
                     base = (x + 2) * ROW0
                     c = 4 * n + 2 * m + h
-                    f0[c, base : base + 8, :] = zero
                     f0[c, base + 8 : base + 24, :] = out[x * 16 : (x + 1) * 16, lanes(h)]
-                    f0[c, base + 24 : base + 32, :] = zero
     for level, (dest, size) in enumerate(((p1, 8), (p2, 4), (p3, 2))):
         for i in range(size):
             for c in range(4):
@@ -155,13 +166,23 @@
                 inc[4 * q + c, pl.ds((2 * i + a) * 16 + b, 8, stride=2), :] = total
 
 
-def inside(f0, tr, inc, ts):
+def inside(f0, tr, inc, ts, t_rr, t_ii):
     re, im = tr[:, :, 0:512], tr[:, :, 512:1024]
     ts[:, :, 0:512] = re
     ts[:, :, 512:1024] = im - re
     ts[:, :, 1024:1536] = re + im
+    offsets = [(dx, dy) for dx in range(-3, 4) for dy in range(-3, 4) if far(dx, dy)]
     for i in range(FIRST):
         leaf(f0, ts, inc, i)
+        for dx, dy in offsets[i::FIRST]:
+            row = (dx + 3) * 7 + dy + 3
+            for c in range(4):
+                re = tr[row, 2:4, lanes(c)]
+                im = tr[row, 2:4, lanes(4 + c)]
+                t_rr[pl.ds(row * 8 + c, 2, stride=392), :] = re
+                t_rr[pl.ds(row * 8 + 4 + c, 2, stride=392), :] = re
+                t_ii[pl.ds(row * 8 + c, 2, stride=392), :] = -im
+                t_ii[pl.ds(row * 8 + 4 + c, 2, stride=392), :] = im
 
 
 def received(axis, r_even, r_odd, lo, hi):
@@ -175,7 +196,10 @@
         hi[c] = jnp.where(me == last, 0.0, jnp.where(even, from_even, from_odd))
 
 
-def strips(r_even, r_odd, msk, p1, p2, p3, x_even, x_odd, ylo, yhi, mlo, mhi):
+def strips(
+    r_odd, r_even, msk, p1, p2, p3, ts, t_rr, t_ii, x_even, x_odd,
+    ylo, yhi, mlo, mhi, xs1, left, right, box2, swp2, out2, box3, swp3, out3, box4, swp4, out4,
+):
     received("col", r_even, r_odd, ylo, yhi)
     even = (lax.axis_index("row") % 2) == 0
     for dest, first in ((mlo, 0), (mhi, 1)):
@@ -194,20 +218,56 @@
                     dest[c, at + 2 : at + 2 + size, :] = level_ref[c, x * 8 : x * 8 + size, :]
                     dest[c, at : at + 2, :] = ylo[c, within + 2 * x : within + 2 * x + 2, :]
                     dest[c, at + 2 + size : at + 4 + size, :] = yhi[c, within + 2 * x : within + 2 * x + 2, :]
-    for c in range(8):
-        lo = mlo[c]
-        hi = mhi[c]
+    both = ((right, mhi), (left, mlo))
+    for c in range(4):
+        for s, (_, src) in enumerate(both):
+            re, im = src[c, 32:56, :], src[4 + c, 32:56, :]
+            for q, part in enumerate((re, im, re + im)):
+                xs1[4 * q + c, s * 24 : s * 24 + 24, :] = part
+    for s, (message, src) in enumerate(both):
+        for c in range(8):
+            message[c, 0:20, :] = src[c, 0:20, :]
+        for c in range(4):
+            acc = {}
+            for xr in range(2):
+                xs = 4 * s + xr
+                for k in range(6):
+                    value = values(xs1, c, pl.ds((2 * s + xr) * 12 + k, 4, stride=2))
+                    for a in range(2):
+                        for b in range(2):
+                            dx, dy = xs - 2 - a, k - 2 - b
+                            if far(dx, dy):
+                                acc[a, b] = add_product(acc.get((a, b)), factors(ts, 1, dx, dy, c), value)
+            for (a, b), sums in acc.items():
+                for q, total in enumerate(complex_sum(sums)):
+                    message[4 * q + c, pl.ds(32 + 8 * a + b, 4, stride=2), :] = total
+    rows = [(6 * s + xr, [(0, 8, src, 56 + 8 * xr)]) for s, (_, src) in enumerate(both) for xr in range(2)]
+    by_box(2, 4, rows, t_rr, t_ii, box2, swp2, out2)
+    for s, (message, src) in enumerate(both):
+        box, swapped, out = ((box3, swp3, out3), (box4, swp4, out4))[s]
+        by_box(3, 2, [(4 * s + xr, [(0, 6, src, 20 + 6 * xr)]) for xr in range(2)], t_rr, t_ii, box, swapped, out)
+        for c in range(8):
+            message[c, 20:24, :] = out[pl.ds(c, 4, stride=8), :]
+            for a in range(2):
+                message[c, 24 + 4 * a : 28 + 4 * a, :] = out2[pl.ds((2 * s + a) * 32 + c, 4, stride=8), :]
+    for c in range(8):
+        lo = left[c]
+        hi = right[c]
         x_even[c] = jnp.where(even, hi, lo).astype(BF16)
         x_odd[c] = jnp.where(even, lo, hi).astype(BF16)
 
 
 def beside_y(
-    r_even, r_odd, msk, f0, p1, p2, p3, inc0, rad, near, tr, ts, base0, near_base, t_rr, t_ii, own1, own2, own3,
-    ylo, yhi, hy, hc, f1, g1, box, swapped, out, cx, ln,
+    r_odd, r_even, msk, f0, p1, p2, p3, inc0, rad, near, ts, t_rr, t_ii, base0, near_base, own1, own2, own3,
+    ylo, yhi, hy, f1, g1, box2, swp2, out2, box3, swp3, out3, cx, ln,
 ):
     received("col", r_even, r_odd, ylo, yhi)
     blocks = []
     zero = jnp.zeros((8, 128), F32)
+    for x in range(N0):
+        kept = msk[x].astype(F32)
+        for c in range(4):
+            cx[c, x * ROW0 + 8 : x * ROW0 + 24, :] = kept[:, lanes(c)]
     for s, src in enumerate((ylo, yhi)):
         for r in range(2):
             both = [
@@ -216,9 +276,7 @@
             blocks.append(jnp.concatenate(both, axis=0))
         touching = blocks[2 * s + 1 - s]
         for c in range(4):
-            hc[s, c, 0:8, :] = zero
-            hc[s, c, 8:24, :] = touching[:, lanes(c)]
-            hc[s, c, 24:32, :] = zero
+            cx[c, pl.ds(7 + 17 * s, 16, stride=ROW0), :] = touching[:, lanes(c)]
     halo = jnp.dot(jnp.concatenate(blocks, axis=0).astype(BF16), rad[...], preferred_element_type=F32)
     halo = halo.astype(BF16).astype(F32)
     for c in range(4):
@@ -228,27 +286,6 @@
                 hy[4 * q + c, n * 32 : n * 32 + 8, :] = zero
                 hy[4 * q + c, n * 32 + 8 : n * 32 + 24, :] = part[16 * n : 16 * n + 16]
                 hy[4 * q + c, n * 32 + 24 : n * 32 + 32, :] = zero
-    for dx in range(-3, 4):
-        for dy in range(-3, 4):
-            if far(dx, dy):
-                row = (dx + 3) * 7 + dy + 3
-                for c in range(4):
-                    re = tr[row, 2:4, lanes(c)]
-                    im = tr[row, 2:4, lanes(4 + c)]
-                    t_rr[pl.ds(row * 8 + c, 2, stride=392), :] = re
-                    t_rr[pl.ds(row * 8 + 4 + c, 2, stride=392), :] = re
-                    t_ii[pl.ds(row * 8 + c, 2, stride=392), :] = -im
-                    t_ii[pl.ds(row * 8 + 4 + c, 2, stride=392), :] = im
-    for c in range(8):
-        base0[c, 0 : FIRST * 32, :] = inc0[c]
-    for i in range(FIRST, 8):
-        leaf(f0, ts, base0, i)
-    for x in range(N0):
-        kept = msk[x].astype(F32)
-        for c in range(4):
-            cx[c, x * ROW0 : x * ROW0 + 8, :] = zero
-            cx[c, x * ROW0 + 8 : x * ROW0 + 24, :] = kept[:, lanes(c)]
-            cx[c, x * ROW0 + 24 : x * ROW0 + 32, :] = zero
     ln[0] = jnp.zeros((16, 1536), BF16)
     ln[17] = jnp.zeros((16, 1536), BF16)
     for dy in range(3):
@@ -256,45 +293,6 @@
             for c in range(4):
                 at = x * ROW0 + 7 + dy
                 ln[x + 1, :, lanes(4 * dy + c)] = cx[c, at : at + 16, :].astype(BF16)
-    total = None
-    for dx in range(3):
-        rows = ln[dx : dx + 16].reshape(N0 * N0, 1536)
-        term = jnp.dot(rows, near[3 * dx : 3 * dx + 3].reshape(1536, 512), preferred_element_type=F32)
-        total = term if total is None else total + term
-    for c in range(4):
-        near_base[c] = total[:, lanes(c)]
-    for s in range(2):
-        for c in range(4):
-            acc = {}
-            for r in range(2):
-                for xs in range(6):
-                    value = values(hy, c, pl.ds((2 * s + r) * 32 + 6 + xs, 8, stride=2))
-                    for a in range(2):
-                        for b in range(2):
-                            dx, dy = xs - 2 - a, 4 * s - 2 + r - b
-                            if far(dx, dy):
-                                acc[a, b] = add_product(acc.get((a, b)), factors(ts, 0, dx, dy, c), value)
-            for (a, b), sums in acc.items():
-                for q, total in enumerate(complex_sum(sums)):
-                    at = pl.ds(16 * a + 14 * s + b, 8, stride=32)
-                    base0[4 * q + c, at, :] = base0[4 * q + c, at, :] + total
-        total = None
-        for dx in range(3):
-            rows = jnp.concatenate([hc[s, c, 7 + dx : 23 + dx, :] for c in range(4)], axis=1).astype(BF16)
-            term = jnp.dot(rows, near[3 * dx + 2 * s], preferred_element_type=F32)
-            total = term if total is None else total + term
-        for c in range(4):
-            at = pl.ds(15 * s, 16, stride=16)
-            near_base[c, at, :] = near_base[c, at, :] + total[:, lanes(c)]
-    for level, size, own, base, inc in ((3, 2, p3, 40, own3), (2, 4, p2, 32, own2)):
-        rows = [
-            (x + 2, [(2, size, own, x * 8), (0, 2, ylo, base + 2 * x), (size + 2, 2, yhi, base + 2 * x)])
-            for x in range(size)
-        ]
-        by_box(level, size, rows, t_rr, t_ii, box, swapped, out)
-        for c in range(8):
-            for x in range(size):
-                inc[c, x * 8 : x * 8 + size, :] = out[pl.ds(x * size * 8 + c, size, stride=8), :]
     for c in range(8):
         for x in range(8):
             base = x * ROWS
@@ -315,25 +313,79 @@
                         parts = (zero, zero, zero)
                     for q, part in enumerate(parts):
                         g1[s, 4 * q + c, at, :] = part
-    for i in range(2):
-        for c in range(4):
-            acc = {}
+    for c in range(8):
+        base0[c, 0 : FIRST * 32, :] = inc0[c]
+
+    def near_term(n):
+        dx, h = n % 3, n // 3
+        rows = ln[dx : dx + 16].reshape(N0 * N0, 1536)
+        weights = near[3 * dx : 3 * dx + 3, :, h * 256 : h * 256 + 256].reshape(1536, 256)
+        term = jnp.dot(rows, weights, preferred_element_type=F32)
+        for q in range(2):
+            if dx == 0:
+                near_base[2 * h + q] = term[:, lanes(q)]
+            else:
+                near_base[2 * h + q] = near_base[2 * h + q] + term[:, lanes(q)]
+
+    def across_y(s, c):
+        acc = {}
+        for r in range(2):
             for xs in range(6):
-                for k in range(6):
-                    if xs in (2, 3) and k in (2, 3):
-                        continue
-                    at = pl.ds((2 * i + xs) * 16 + k % 2, 8, stride=2)
-                    value = [g1[k // 2, 4 * q + c, at, :] for q in range(3)]
-                    for a in range(2):
-                        for b in range(2):
-                            dx, dy = xs - 2 - a, k - 2 - b
-                            if far(dx, dy):
-                                acc[a, b] = add_product(acc.get((a, b)), factors(ts, 1, dx, dy, c), value)
-            for (a, b), sums in acc.items():
-                for q, total in enumerate(complex_sum(sums)):
-                    for h in range(2):
-                        at = pl.ds((2 * (i + 2 * h) + a) * 8 + b, 4, stride=2)
-                        own1[4 * q + c, at, :] = total[4 * h : 4 * h + 4]
+                value = values(hy, c, pl.ds((2 * s + r) * 32 + 6 + xs, 8, stride=2))
+                for a in range(2):
+                    for b in range(2):
+                        dx, dy = xs - 2 - a, 4 * s - 2 + r - b
+                        if far(dx, dy):
+                            acc[a, b] = add_product(acc.get((a, b)), factors(ts, 0, dx, dy, c), value)
+        for (a, b), sums in acc.items():
+            for q, total in enumerate(complex_sum(sums)):
+                at = pl.ds(16 * a + 14 * s + b, 8, stride=32)
+                base0[4 * q + c, at, :] = base0[4 * q + c, at, :] + total
+
+    def middle(i, c):
+        acc = {}
+        for xs in range(6):
+            for k in range(6):
+                if xs in (2, 3) and k in (2, 3):
+                    continue
+                at = pl.ds((2 * i + xs) * 16 + k % 2, 8, stride=2)
+                value = [g1[k // 2, 4 * q + c, at, :] for q in range(3)]
+                for a in range(2):
+                    for b in range(2):
+                        dx, dy = xs - 2 - a, k - 2 - b
+                        if far(dx, dy):
+                            acc[a, b] = add_product(acc.get((a, b)), factors(ts, 1, dx, dy, c), value)
+        for (a, b), sums in acc.items():
+            for q, total in enumerate(complex_sum(sums)):
+                for h in range(2):
+                    at = pl.ds((2 * (i + 2 * h) + a) * 8 + b, 4, stride=2)
+                    own1[4 * q + c, at, :] = total[4 * h : 4 * h + 4]
+
+    def small(level):
+        size, own, base, inc = {2: (4, p2, 32, own2), 3: (2, p3, 40, own3)}[level]
+        box, swapped, out = {2: (box2, swp2, out2), 3: (box3, swp3, out3)}[level]
+        rows = [
+            (x + 2, [(2, size, own, x * 8), (0, 2, ylo, base + 2 * x), (size + 2, 2, yhi, base + 2 * x)])
+            for x in range(size)
+        ]
+        by_box(level, size, rows, t_rr, t_ii, box, swapped, out)
+        for c in range(8):
+            for x in range(size):
+                inc[c, x * 8 : x * 8 + size, :] = out[pl.ds(x * size * 8 + c, size, stride=8), :]
+
+    for n in range(6):
+        near_term(n)
+        if n < 4:
+            for i in range(2):
+                middle(i, n)
+        else:
+            for c in range(4):
+                across_y(n - 4, c)
+        if n in (1, 2):
+            small(n + 1)
+        if n == 3:
+            for i in range(FIRST, 8):
+                leaf(f0, ts, base0, i)
 
 
 def add_parent(inc, parent, shf, level, size):
@@ -387,8 +439,8 @@
 
 
 def downward(
-    cnt, inc0, near_base, t_rr, t_ii, own1, own2, own3, x_even, x_odd, rad, rec, near, ts, shf,
-    field, xlo, xhi, hc, hx, xs1, box, swapped, out, tot, inc1, inc2, inc3, half,
+    count, inc0, near_base, own1, own2, own3, x_even, x_odd, rad, rec, near, ts, shf,
+    field, xlo, xhi, hc, hx, tot, inc1, inc2, inc3, half,
 ):
     received("row", x_even, x_odd, xlo, xhi)
     sides = []
@@ -403,43 +455,26 @@
         re, im = halo[:, lanes(c)], halo[:, lanes(4 + c)]
         for q, part in enumerate((re, im, re + im)):
             hx[4 * q + c] = part
-        for s, src in enumerate((xlo, xhi)):
-            re, im = src[c, 32:56, :], src[4 + c, 32:56, :]
-            for q, part in enumerate((re, im, re + im)):
-                xs1[4 * q + c, s * 24 : s * 24 + 24, :] = part
-
-    for level, size, base, own, inc in ((3, 2, 20, own3, inc3), (2, 4, 56, own2, inc2)):
-        wide = size + 4
-        rows = [
-            (xe + xr, [(0, wide, src, base + wide * xr)]) for src, xe in ((xlo, 0), (xhi, size + 2)) for xr in range(2)
-        ]
-        by_box(level, size, rows, t_rr, t_ii, box, swapped, out)
-        for c in range(8):
-            for x in range(size):
-                at = slice(x * 8, x * 8 + size)
-                inc[c, at, :] = own[c, at, :] + out[pl.ds(x * size * 8 + c, size, stride=8), :]
+
+    for c in range(8):
+        for x in range(2):
+            at = slice(x * 8, x * 8 + 2)
+            both = slice(20 + 2 * x, 22 + 2 * x)
+            inc3[c, at, :] = own3[c, at, :] + xlo[c, both, :] + xhi[c, both, :]
+        for x in range(4):
+            at = slice(x * 8, x * 8 + 4)
+            side = (xlo, xhi)[x // 2]
+            inc2[c, at, :] = own2[c, at, :] + side[c, 24 + 4 * (x % 2) : 28 + 4 * (x % 2), :]
+        for x in range(8):
+            at = slice(x * 8, x * 8 + 8)
+            value = own1[c, at, :]
+            if x in (0, 1, 6, 7):
+                value = value + (xlo, xhi)[x // 6][c, 32 + 8 * (x % 2) : 40 + 8 * (x % 2), :]
+            inc1[c, at, :] = value
     add_parent(inc2, inc3, shf, 2, 4)
-    for c in range(8):
-        inc1[c] = own1[c]
-    for s in range(2):
-        for c in range(4):
-            acc = {}
-            for xr in range(2):
-                xs = 4 * s + xr
-                for k in range(6):
-                    value = values(xs1, c, pl.ds((2 * s + xr) * 12 + k, 4, stride=2))
-                    for a in range(2):
-                        for b in range(2):
-                            dx, dy = xs - 2 - a, k - 2 - b
-                            if far(dx, dy):
-                                acc[a, b] = add_product(acc.get((a, b)), factors(ts, 1, dx, dy, c), value)
-            for (a, b), sums in acc.items():
-                at = pl.ds((6 * s + a) * 8 + b, 4, stride=2)
-                for q, total in enumerate(complex_sum(sums)):
-                    inc1[4 * q + c, at, :] = inc1[4 * q + c, at, :] + total
     add_parent(inc1, inc2, shf, 1, 8)
 
-    for x in range(N0):
+    def leaf_columns(x):
         for b in range(2):
             row = slice(2 * (x % 2) + b, 2 * (x % 2) + b + 1)
             at = pl.ds(x * 16 + b, 8, stride=2)
@@ -450,7 +485,8 @@
                 t_im = shf[0, row, lanes(4 + c)]
                 tot[c, at, :] = inc0[c, at, :] + (t_re * q_re + t_im * q_im)
                 tot[4 + c, at, :] = inc0[4 + c, at, :] + (t_re * q_im - t_im * q_re)
-    for s in range(2):
+
+    def from_x_halo(s):
         for c in range(4):
             acc = {}
             for xr in range(2):
@@ -466,32 +502,40 @@
                 at = pl.ds((14 * s + a) * 16 + b, 8, stride=2)
                 for q, total in enumerate(complex_sum(sums)):
                     tot[4 * q + c, at, :] = tot[4 * q + c, at, :] + total
-    for c in range(8):
-        half[:, lanes(c)] = tot[c].astype(BF16)
-    side = []
-    for s in range(2):
+
+    def near_side(s):
         total = None
         for dy in range(3):
             rows = jnp.concatenate([hc[s, c, 1 + dy : 17 + dy, :] for c in range(4)], axis=1).astype(BF16)
             term = jnp.dot(rows, near[6 * s + dy], preferred_element_type=F32)
             total = term if total is None else total + term
-        side.append(total)
+        return total
+
+    for x in range(N0):
+        leaf_columns(x)
+    for s in range(2):
+        from_x_halo(s)
+    for c in range(8):
+        half[:, lanes(c)] = tot[c].astype(BF16)
+    sides = [near_side(s) for s in range(2)]
     total = jnp.dot(half[...], rec[...], preferred_element_type=F32)
     for x in range(N0):
-        here = slice(x * 16, (x + 1) * 16)
-        result = total[here] + jnp.concatenate([near_base[c, here, :] for c in range(4)], axis=1)
-        if x in (0, N0 - 1):
-            result = result + side[x // (N0 - 1)]
-        field[x] = jnp.where(occupied_rows(cnt, x), result, 0.0).astype(BF16)
-
-
-def call(kernel, outs, scratch, flops, *args):
+        own = slice(x * 16, x * 16 + 16)
+        for c in range(4):
+            result = total[own, lanes(c)] + near_base[c, own, :]
+            if x in (0, N0 - 1):
+                result = result + sides[x // (N0 - 1)][:, lanes(c)]
+            field[x, :, lanes(c)] = jnp.where(occupied(count[own, :], c), result, 0.0).astype(BF16)
+
+
+def call(kernel, outs, scratch, flops, *args, aliases=None):
     place = pl.BlockSpec(memory_space=pltpu.VMEM)
     return pl.pallas_call(
         kernel,
         out_shape=outs,
         in_specs=[place] * len(args),
         out_specs=[place] * len(outs),
+        input_output_aliases=aliases or {},
         scratch_shapes=scratch,
         compiler_params=pltpu.CompilerParams(vmem_limit_bytes=16 * 1024 * 1024),
         cost_estimate=pl.CostEstimate(flops=flops, bytes_accessed=1 << 20, transcendentals=0),
@@ -510,12 +554,18 @@
 def shards(currents, counts, radiate, receive, near_blocks, translate, shift):
     mem = pltpu.VMEM
     factor = jnp.transpose(translate, (1, 0, 2))
-    ys, xs = mem((8, SY, 128), F32), mem((8, SX, 128), F32)
-    (first,) = call(opening, [shape((8, 128), F32)], [], 10**13)
-    masked, f0, p1, p2, p3, m_even, m_odd = call(
+    ys, xs, strip = mem((8, SY, 128), F32), mem((8, MX, 128), F32), mem((8, SX, 128), F32)
+    (f0,) = call(opening, [shape((12, 20 * ROW0, 128), F32)], [], 10**13)
+    masked, c0, count = call(
+        mask,
+        [shape((16, 16, 512), BF16), shape((4, 256, 128), F32), shape((256, 128), F32)],
+        [],
+        1,
+        currents, counts,
+    )
+    f0, p1, p2, p3, m_odd, m_even = call(
         upward,
         [
-            shape((16, 16, 512), BF16),
             shape((12, 20 * ROW0, 128), F32),
             shape((8, 64, 128), F32),
             shape((8, 32, 128), F32),
@@ -523,54 +573,63 @@
             shape((8, SY, 128), BF16),
             shape((8, SY, 128), BF16),
         ],
-        [mem((4, 256, 128), F32), ys, ys],
+        [ys, ys],
         10**12,
-        first, currents, counts, radiate, shift,
+        f0, masked, c0, radiate, shift,
+        aliases={0: 0},
     )
+    r_odd = swap(m_odd, "col", 1)
     r_even = swap(m_even, "col", 0)
-    r_odd = swap(m_odd, "col", 1)
-    inc0, sums = call(
+    inc0, sums, t_rr, t_ii = call(
         inside,
-        [shape((8, 32 * FIRST, 128), F32), shape((49, 4, 1536), F32)],
+        [
+            shape((8, 32 * FIRST, 128), F32), shape((49, 4, 1536), F32),
+            shape((784, 128), F32), shape((784, 128), F32),
+        ],
         [],
         4 * 10**9,
         f0, factor,
     )
-    r_even, r_odd, inc0 = lax.optimization_barrier((r_even, r_odd, inc0))
+    r_odd, r_even, inc0 = lax.optimization_barrier((r_odd, r_even, inc0))
     s_even, s_odd = call(
         strips,
-        [shape((8, SX, 128), BF16)] * 2,
-        [ys, ys, xs, xs],
+        [shape((8, MX, 128), BF16)] * 2,
+        [
+            ys, ys, strip, strip, mem((12, 48, 128), F32), xs, xs,
+            mem((512, 128), F32), mem((512, 128), F32), mem((128, 128), F32),
+            mem((288, 128), F32), mem((288, 128), F32), mem((32, 128), F32),
+            mem((288, 128), F32), mem((288, 128), F32), mem((32, 128), F32),
+        ],
         10**7,
-        r_even, r_odd, masked, p1, p2, p3,
+        r_odd, r_even, masked, p1, p2, p3, sums, t_rr, t_ii,
     )
     x_even = swap(s_even, "row", 0)
     x_odd = swap(s_odd, "row", 1)
-    inc0, near_sum, t_rr, t_ii, own1, own2, own3 = call(
+    inc0, near_sum, own1, own2, own3 = call(
         beside_y,
         [
-            shape((8, 256, 128), F32), shape((4, 256, 128), F32), shape((784, 128), F32), shape((784, 128), F32),
+            shape((8, 256, 128), F32), shape((4, 256, 128), F32),
             shape((8, 64, 128), F32), shape((8, 32, 128), F32), shape((8, 16, 128), F32),
         ],
         [
-            ys, ys, mem((12, 128, 128), F32), mem((2, 4, 32, 128), F32), mem((8, 8 * ROWS, 128), F32),
-            mem((3, 12, 128, 128), F32), mem((512, 128), F32), mem((512, 128), F32), mem((128, 128), F32),
+            ys, ys, mem((12, 128, 128), F32), mem((8, 8 * ROWS, 128), F32), mem((3, 12, 128, 128), F32),
+            mem((512, 128), F32), mem((512, 128), F32), mem((128, 128), F32),
+            mem((288, 128), F32), mem((288, 128), F32), mem((32, 128), F32),
             mem((4, 16 * ROW0, 128), F32), mem((18, 16, 1536), BF16),
         ],
         10**9,
-        r_even, r_odd, masked, f0, p1, p2, p3, inc0, radiate, near_blocks, factor, sums,
+        r_odd, r_even, masked, f0, p1, p2, p3, inc0, radiate, near_blocks, sums, t_rr, t_ii,
     )
     (field,) = call(
         downward,
         [shape((16, 16, 512), BF16)],
         [
-            xs, xs, mem((2, 4, 24, 128), F32), mem((12, 128, 128), F32), mem((12, 48, 128), F32),
-            mem((512, 128), F32), mem((512, 128), F32), mem((128, 128), F32),
+            xs, xs, mem((2, 4, 24, 128), F32), mem((12, 128, 128), F32),
             mem((8, 256, 128), F32), mem((8, 64, 128), F32), mem((8, 32, 128), F32), mem((8, 16, 128), F32),
             mem((256, 1024), BF16),
         ],
         3 * 10**9,
-        counts, inc0, near_sum, t_rr, t_ii, own1, own2, own3, x_even, x_odd,
+        count, inc0, near_sum, own1, own2, own3, x_even, x_odd,
         radiate, receive, near_blocks, sums, shift,
     )
     return field

time: 19.9 us -> 18.7 us (0.940)
  waiting for transfers between devices: 0.72 us -> 0.16 us
  Pallas kernels: 11 us -> 10.5 us
  local copies, waits for them, and re-layouts: 1.29 us -> 1.05 us
    ppermute x4, waiting for transfers between devices: 0.72 us -> 0.16 us  [swap(): return lax.ppermute(value, ('row', 'col'), swap_perm(axis, odd))]
    pallas_call x6 -> x7, Pallas kernels: 11 us -> 10.5 us  [call(): pl.pallas_call(kernel, out_shape=outs, in_specs=[place] * len(args), out_...]
    unnamed x16, local copies, waits for them, and re-layouts: 1.29 us -> 1.05 us
where the time goes in v2:
time: 18.7 us; the launch traced here: 18.6 us
  Pallas kernels  10.5 us (56%)
  starting transfers between devices  6.78 us (36%)
  local copies, waits for them, and re-layouts  1.05 us (6%)
    pallas_call x7, Pallas kernels, call(): pl.pallas_call(kernel, out_shape=outs, in_specs=[place] * len(args), out_...  10.5 us
    ppermute x4, starting transfers between devices, swap(): return lax.ppermute(value, ('row', 'col'), swap_perm(axis, odd))  6.78 us
    unnamed x16, local copies, waits for them, and re-layouts  1.05 us
  transfers between devices with their start and end apart: 4, of which 1 were waited for; matrix products, arithmetic and copies ran while one was open for 0% of the time, Pallas kernels for 35%

profile of v2, /device:TPU:6, one launch (start us, length us, event | category | flops | bytes accessed | tf_op | source)
XLA Modules:
  0.0 18.6 jit_solution(11789955416350801777)
XLA Ops:
  0.0 0.0 copy-start.1
  0.0 0.0 copy-start.2
  0.0 0.0 copy-start
  0.0 0.0 copy-start.5
  0.0 0.1 shard_map.74.f0_zero
  0.1 0.8 %copy-done.1 = bf16[16,16,512]{2,1,0:T(8,128)(2,1)S(1)} copy-done((bf16[16,16,512]{2,1,0:T(8,128)(2,1)S(1)}, bf16[16,16,512]{2,1,0:T(8,128)(2,1)}, u32[]{:S(2)}) %copy-start.1) | copy-done | bytes 262168
  1.0 0.0 copy-done.2
  1.0 0.2 shard_map.73
  1.1 0.2 %copy-done = bf16[512,1024]{1,0:T(8,128)(2,1)S(1)} copy-done((bf16[512,1024]{1,0:T(8,128)(2,1)S(1)}, bf16[512,1024]{1,0:T(8,128)(2,1)}, u32[]{:S(2)}) %copy-start) | copy-done | bytes 1048600
  1.3 0.0 copy-done.5
  1.3 0.0 copy-start.4
  1.3 0.8 %shard_map.75 = (f32[12,640,128]{2,1,0:T(8,128)S(1)}, f32[8,64,128]{2,1,0:T(8,128)S(1)}, f32[8,32,128]{2,1,0:T(8,128)S(1)}, f32[8,16,128]{2,1,0:T(8,128)S(1)}, b...) custom-call(f32[12,640,128]{2,1,0:T(8,128)S(1)} %shard_map.74.f0_zero, ...), custom_call_target="tpu_custom_call", output_to_operand_aliasing={{0}: (0, {})} | custom-call | flops 999999995904 | bytes 1048576 | tf_op jit(solution)/shard_map/pallas_call | solution.py:533
  2.2 2.0 %collective-permute-start = (bf16[8,48,128]{2,1,0:T(8,128)(2,1)S(1)}, bf16[8,48,128]{2,1,0:T(8,128)(2,1)S(1)}, u32[]{:S(2)}, u32[]{:S(2)}) collective-permute-start(bf16[8,48,128]{2,1,0:T(8,128)(2,1)S(1)} %get-tuple-element.31), channel_id=1, source_target_pairs={{0,8},{1,2},{2,1},{3,4},{4,3},{5,6},{6,5},{7,15},{8,0},{9,10},{10,... | collective-permute-start | bytes 294920 | tf_op jit(solution)/shard_map/ppermute | solution.py:551
  4.2 0.0 collective-permute-start.1
  4.2 0.0 slice-start
  4.2 0.0 copy-done.4
  4.2 0.0 slice-start.1
  4.2 2.7 %shard_map.76 = (f32[8,224,128]{2,1,0:T(8,128)S(1)}, f32[49,4,1536]{2,1,0:T(4,128)S(1)}, f32[784,128]{1,0:T(8,128)S(1)}, f32[784,128]{1,0:T(8,128)S(1)}) custom-call(f32[12,640,128]{2,1,0:T(8,128)S(1)} %get-tuple-element.33.f0, f32[49,4,1024]{2,1,0:T(4,128)S(1)} %bitcast.3), custom_call_target="tpu_custom_call" | custom-call | flops 4000000000 | bytes 1048576 | tf_op jit(solution)/shard_map/pallas_call | solution.py:533
  6.8 0.0 collective-permute-done.r_odd
  6.9 0.0 collective-permute-done.1.r_even
  6.9 0.7 %shard_map.78 = (bf16[8,48,128]{2,1,0:T(8,128)(2,1)S(1)}, bf16[8,48,128]{2,1,0:T(8,128)(2,1)S(1)}) custom-call(bf16[8,48,128]{2,1,0:T(8,128)(2,1)S(1)} %collective-permute-done.r_odd, bf16[8,48,128]{2,1,0:T(8,128)(2,1)S(1)} %collective-permute-done.1.r_even, bf16[16,16,512]{2,1,0:T(8,128)(2,1)S(1)} %get-tuple-element.29.msk, ...), custom_call_target="tpu_custom_call" | custom-call | flops 10000000 | bytes 1048576 | tf_op jit(solution)/shard_map/pallas_call | solution.py:533
  7.5 2.0 %collective-permute-start.2 = (bf16[8,48,128]{2,1,0:T(8,128)(2,1)S(1)}, bf16[8,48,128]{2,1,0:T(8,128)(2,1)S(1)}, u32[]{:S(2)}, u32[]{:S(2)}) collective-permute-start(bf16[8,48,128]{2,1,0:T(8,128)(2,1)S(1)} %get-tuple-element.49), channel_id=1, source_target_pairs={{0,8},{1,9},{2,10},{3,11},{4,12},{5,13},{6,14},{7,15},{8,0},{9,1},... | collective-permute-start | bytes 294920 | tf_op jit(solution)/shard_map/ppermute | solution.py:551
  9.5 0.0 copy-start.3
  9.5 2.8 %collective-permute-start.3 = (bf16[8,48,128]{2,1,0:T(8,128)(2,1)S(1)}, bf16[8,48,128]{2,1,0:T(8,128)(2,1)S(1)}, u32[]{:S(2)}, u32[]{:S(2)}) collective-permute-start(bf16[8,48,128]{2,1,0:T(8,128)(2,1)S(1)} %get-tuple-element.50), channel_id=1, source_target_pairs={{0,1},{1,0},{2,3},{3,2},{4,5},{5,4},{6,7},{7,6},{8,16},{9,17},{10,... | collective-permute-start | bytes 294920 | tf_op jit(solution)/shard_map/ppermute | solution.py:551
  12.3 0.0 slice-done
  12.3 0.0 slice-done.1
  12.3 3.8 %shard_map.77 = (f32[8,256,128]{2,1,0:T(8,128)S(1)}, f32[4,256,128]{2,1,0:T(8,128)S(1)}, f32[8,64,128]{2,1,0:T(8,128)S(1)}, f32[8,32,128]{2,1,0:T(8,128)S(1)}, f32[8,16,128]{2,1,0:T(8,128)S(1)}) custom-call(bf16[8,48,128]{2,1,0:T(8,128)(2,1)S(1)} %collective-permute-done.r_odd, bf16[8,48,128]{2,1,0:T(8,128)(2,1)S(1)} %collective-permute-done.1.r_even, ...), custom_call_target="tpu_custom_call" | custom-call | flops 1000000000 | bytes 1048576 | tf_op jit(solution)/shard_map/pallas_call | solution.py:533
  16.1 0.0 collective-permute-done.2.x_even
  16.1 0.1 collective-permute-done.3.x_odd
  16.3 0.0 copy-done.3
  16.3 2.3 %shard_map.79 = bf16[16,16,512]{2,1,0:T(8,128)(2,1)} custom-call(f32[256,128]{1,0:T(8,128)S(1)} %get-tuple-element.28.count, f32[8,256,128]{2,1,0:T(8,128)S(1)} %get-tuple-element.44.inc0, f32[4,256,128]{2,1,0:T(8,128)S(1)} %get-tuple-element.45.near_base, f32[8,64,128]{2,1,0:T(8,128)S(1)} %get-tuple-element.46.own1, ...), custom_call_target="tpu_custom_call" | custom-call | flops 3000000000 | bytes 1048576 | tf_op jit(solution)/shard_map/pallas_call | solution.py:533
  (1 shorter events, 0.0 us)
Async XLA Ops:
  0.0 0.9 %copy-start.1 = (bf16[16,16,512]{2,1,0:T(8,128)(2,1)S(1)}, bf16[16,16,512]{2,1,0:T(8,128)(2,1)}, u32[]{:S(2)}) copy-start(bf16[16,16,512]{2,1,0:T(8,128)(2,1)} %cur.1) | copy-start | bytes 786436
  0.0 1.0 %copy-start.2 = (s32[16,16]{1,0:T(8,128)S(1)}, s32[16,16]{1,0:T(8,128)}, u32[]{:S(2)}) copy-start(s32[16,16]{1,0:T(8,128)} %cnt.1) | copy-start | bytes 3076
  0.0 1.3 %copy-start = (bf16[512,1024]{1,0:T(8,128)(2,1)S(1)}, bf16[512,1024]{1,0:T(8,128)(2,1)}, u32[]{:S(2)}) copy-start(bf16[512,1024]{1,0:T(8,128)(2,1)} %rad.5) | copy-start | bytes 3145732
  0.0 1.3 %copy-start.5 = (f32[3,4,1024]{2,1,0:T(4,128)S(1)}, f32[3,4,1024]{2,1,0:T(4,128)}, u32[]{:S(2)}) copy-start(f32[3,4,1024]{2,1,0:T(4,128)} %shf.3) | copy-start | bytes 147460
  1.3 2.8 %copy-start.4 = (f32[4,49,1024]{2,0,1:T(4,128)S(1)}, f32[4,49,1024]{2,0,1:T(4,128)}, u32[]{:S(2)}) copy-start(f32[4,49,1024]{2,0,1:T(4,128)} %param.12) | copy-start | bytes 2408452
  2.2 4.7 %collective-permute-start = (bf16[8,48,128]{2,1,0:T(8,128)(2,1)S(1)}, bf16[8,48,128]{2,1,0:T(8,128)(2,1)S(1)}, u32[]{:S(2)}, u32[]{:S(2)}) collective-permute-start(bf16[8,48,128]{2,1,0:T(8,128)(2,1)S(1)} %get-tuple-element.31), channel_id=1, source_target_pairs={{0,8},{1,2},{2,1},{3,4},{4,3},{5,6},{6,5},{7,15},{8,0},{9,10},{10,... | collective-permute-start | bytes 294920 | tf_op jit(solution)/shard_map/ppermute | solution.py:551
  4.2 2.7 %collective-permute-start.1 = (bf16[8,48,128]{2,1,0:T(8,128)(2,1)S(1)}, bf16[8,48,128]{2,1,0:T(8,128)(2,1)S(1)}, u32[]{:S(2)}, u32[]{:S(2)}) collective-permute-start(bf16[8,48,128]{2,1,0:T(8,128)(2,1)S(1)} %get-tuple-element.32), channel_id=1, source_target_pairs={{0,1},{1,0},{2,3},{3,2},{4,5},{5,4},{6,7},{7,6},{8,9},{9,8},{10,11... | collective-permute-start | bytes 294920 | tf_op jit(solution)/shard_map/ppermute | solution.py:551
  4.2 8.2 %slice-start = ((s8[4718592]{0:T(1024)(128)(4,1)}), s8[4194304]{0:T(1024)(128)(4,1)S(1)}, s32[]{:S(2)}) async-start(s8[4718592]{0:T(1024)(128)(4,1)} %bitcast.1), calls=%async_computation | async-start | bytes 8388608
  4.2 8.2 %slice-start.1 = ((s8[4718592]{0:T(1024)(128)(4,1)}), s8[524288]{0:T(1024)(128)(4,1)S(1)}, s32[]{:S(2)}) async-start(s8[4718592]{0:T(1024)(128)(4,1)} %bitcast.1), calls=%async_computation.1 | async-start | bytes 1048576
  7.5 8.6 %collective-permute-start.2 = (bf16[8,48,128]{2,1,0:T(8,128)(2,1)S(1)}, bf16[8,48,128]{2,1,0:T(8,128)(2,1)S(1)}, u32[]{:S(2)}, u32[]{:S(2)}) collective-permute-start(bf16[8,48,128]{2,1,0:T(8,128)(2,1)S(1)} %get-tuple-element.49), channel_id=1, source_target_pairs={{0,8},{1,9},{2,10},{3,11},{4,12},{5,13},{6,14},{7,15},{8,0},{9,1},... | collective-permute-start | bytes 294920 | tf_op jit(solution)/shard_map/ppermute | solution.py:551
  9.5 6.7 %copy-start.3 = (bf16[1024,512]{1,0:T(8,128)(2,1)S(1)}, bf16[1024,512]{1,0:T(8,128)(2,1)}, u32[]{:S(2)}) copy-start(bf16[1024,512]{1,0:T(8,128)(2,1)} %rec.1) | copy-start | bytes 3145732
  9.5 6.7 %collective-permute-start.3 = (bf16[8,48,128]{2,1,0:T(8,128)(2,1)S(1)}, bf16[8,48,128]{2,1,0:T(8,128)(2,1)S(1)}, u32[]{:S(2)}, u32[]{:S(2)}) collective-permute-start(bf16[8,48,128]{2,1,0:T(8,128)(2,1)S(1)} %get-tuple-element.50), channel_id=1, source_target_pairs={{0,1},{1,0},{2,3},{3,2},{4,5},{5,4},{6,7},{7,6},{8,16},{9,17},{10,... | collective-permute-start | bytes 294920 | tf_op jit(solution)/shard_map/ppermute | solution.py:551

commit v3 on v2

--- a/solution.py
+++ b/solution.py
@@ -98,7 +98,7 @@
             jnp.dot(lhs, rad[:, n : n + 256], preferred_element_type=F32).astype(BF16).astype(F32)
             for n in (256 * m, 512 + 256 * m)
         ]
-        for n, out in enumerate((re, im, re + im)):
+        for n, out in enumerate((re, im)):
             for h in range(2):
                 for x in range(N0):
                     base = (x + 2) * ROW0
@@ -166,11 +166,15 @@
                 inc[4 * q + c, pl.ds((2 * i + a) * 16 + b, 8, stride=2), :] = total
 
 
-def inside(f0, tr, inc, ts, t_rr, t_ii):
+def inside(f0_in, tr, f0, inc, ts, t_rr, t_ii):
     re, im = tr[:, :, 0:512], tr[:, :, 512:1024]
     ts[:, :, 0:512] = re
     ts[:, :, 512:1024] = im - re
     ts[:, :, 1024:1536] = re + im
+    for c in range(4):
+        for x in range(N0):
+            own = slice((x + 2) * ROW0 + 8, (x + 2) * ROW0 + 24)
+            f0[8 + c, own, :] = f0[c, own, :] + f0[4 + c, own, :]
     offsets = [(dx, dy) for dx in range(-3, 4) for dy in range(-3, 4) if far(dx, dy)]
     for i in range(FIRST):
         leaf(f0, ts, inc, i)
@@ -446,7 +450,7 @@
     sides = []
     for s, src in enumerate((xlo, xhi)):
         for xr in range(2):
-            sides.append(jnp.concatenate([src[4 * xr + c, 0:32, :] for c in range(4)], axis=1))
+            sides.append(jnp.concatenate([src[4 * xr + c, 0:24, :] for c in range(4)], axis=1))
         for c in range(4):
             hc[s, c, 0:24, :] = src[4 * (1 - s) + c, 0:24, :]
     halo = jnp.dot(jnp.concatenate(sides, axis=0).astype(BF16), rad[...], preferred_element_type=F32)
@@ -492,7 +496,7 @@
             for xr in range(2):
                 xs = 4 * s + xr
                 for k in range(6):
-                    value = values(hx, c, pl.ds((2 * s + xr) * 32 + k, 8, stride=2))
+                    value = values(hx, c, pl.ds((2 * s + xr) * 24 + k, 8, stride=2))
                     for a in range(2):
                         for b in range(2):
                             dx, dy = xs - 2 - a, k - 2 - b
@@ -580,15 +584,17 @@
     )
     r_odd = swap(m_odd, "col", 1)
     r_even = swap(m_even, "col", 0)
-    inc0, sums, t_rr, t_ii = call(
+    f0, inc0, sums, t_rr, t_ii = call(
         inside,
         [
+            shape((12, 20 * ROW0, 128), F32),
             shape((8, 32 * FIRST, 128), F32), shape((49, 4, 1536), F32),
             shape((784, 128), F32), shape((784, 128), F32),
         ],
         [],
         4 * 10**9,
         f0, factor,
+        aliases={0: 0},
     )
     r_odd, r_even, inc0 = lax.optimization_barrier((r_odd, r_even, inc0))
     s_even, s_odd = call(
@@ -624,7 +630,7 @@
         downward,
         [shape((16, 16, 512), BF16)],
         [
-            xs, xs, mem((2, 4, 24, 128), F32), mem((12, 128, 128), F32),
+            xs, xs, mem((2, 4, 24, 128), F32), mem((12, 96, 128), F32),
             mem((8, 256, 128), F32), mem((8, 64, 128), F32), mem((8, 32, 128), F32), mem((8, 16, 128), F32),
             mem((256, 1024), BF16),
         ],

time: 18.7 us -> 18.6 us (level)
  no operation moved by 1% of the time
where the time goes in v3:
time: 18.6 us; the launch traced here: 18.5 us
  Pallas kernels  10.5 us (56%)
  starting transfers between devices  6.73 us (36%)
  local copies, waits for them, and re-layouts  1.05 us (6%)
    pallas_call x7, Pallas kernels, call(): pl.pallas_call(kernel, out_shape=outs, in_specs=[place] * len(args), out_...  10.5 us
    ppermute x4, starting transfers between devices, swap(): return lax.ppermute(value, ('row', 'col'), swap_perm(axis, odd))  6.73 us
    unnamed x16, local copies, waits for them, and re-layouts  1.05 us
  transfers between devices with their start and end apart: 4, of which 1 were waited for; matrix products, arithmetic and copies ran while one was open for 0% of the time, Pallas kernels for 35%

profile of v3, /device:TPU:6, one launch (start us, length us, event | category | flops | bytes accessed | tf_op | source)
XLA Modules:
  0.0 18.5 jit_solution(18012876036522349264)
XLA Ops:
  0.0 0.0 copy-start.1
  0.0 0.0 copy-start.2
  0.0 0.0 copy-start
  0.0 0.0 copy-start.5
  0.0 0.1 shard_map.74.f0_zero
  0.1 0.8 %copy-done.1 = bf16[16,16,512]{2,1,0:T(8,128)(2,1)S(1)} copy-done((bf16[16,16,512]{2,1,0:T(8,128)(2,1)S(1)}, bf16[16,16,512]{2,1,0:T(8,128)(2,1)}, u32[]{:S(2)}) %copy-start.1) | copy-done | bytes 262168
  1.0 0.0 copy-done.2
  1.0 0.2 shard_map.73
  1.1 0.2 %copy-done = bf16[512,1024]{1,0:T(8,128)(2,1)S(1)} copy-done((bf16[512,1024]{1,0:T(8,128)(2,1)S(1)}, bf16[512,1024]{1,0:T(8,128)(2,1)}, u32[]{:S(2)}) %copy-start) | copy-done | bytes 1048600
  1.3 0.0 copy-done.5
  1.3 0.0 copy-start.4
  1.3 0.8 %shard_map.75 = (f32[12,640,128]{2,1,0:T(8,128)S(1)}, f32[8,64,128]{2,1,0:T(8,128)S(1)}, f32[8,32,128]{2,1,0:T(8,128)S(1)}, f32[8,16,128]{2,1,0:T(8,128)S(1)}, b...) custom-call(f32[12,640,128]{2,1,0:T(8,128)S(1)} %shard_map.74.f0_zero, ...), custom_call_target="tpu_custom_call", output_to_operand_aliasing={{0}: (0, {})} | custom-call | flops 999999995904 | bytes 1048576 | tf_op jit(solution)/shard_map/pallas_call | solution.py:537
  2.1 2.0 %collective-permute-start = (bf16[8,48,128]{2,1,0:T(8,128)(2,1)S(1)}, bf16[8,48,128]{2,1,0:T(8,128)(2,1)S(1)}, u32[]{:S(2)}, u32[]{:S(2)}) collective-permute-start(bf16[8,48,128]{2,1,0:T(8,128)(2,1)S(1)} %get-tuple-element.32), channel_id=1, source_target_pairs={{0,8},{1,2},{2,1},{3,4},{4,3},{5,6},{6,5},{7,15},{8,0},{9,10},{10,... | collective-permute-start | bytes 294920 | tf_op jit(solution)/shard_map/ppermute | solution.py:555
  4.1 0.0 collective-permute-start.1
  4.1 0.0 slice-start
  4.1 0.0 copy-done.4
  4.1 0.0 slice-start.1
  4.1 2.7 %shard_map.76 = (f32[12,640,128]{2,1,0:T(8,128)S(1)}, f32[8,224,128]{2,1,0:T(8,128)S(1)}, f32[49,4,1536]{2,1,0:T(4,128)S(1)}, f32[784,128]{1,0:T(8,128)S(1)}, f32[784,128]{1,0:T(8,128)S(1)}) custom-call(f32[12,640,128]{2,1,0:T(8,128)S(1)} %get-tuple-element.34.f0_in, f32[49,4,1024]{2,1,0:T(4,128)S(1)} %bitcast.3), custom_call_target="tpu_custom_call", output_to_operand_aliasing={{0}: (0, {})} | custom-call | flops 4000000000 | bytes 1048576 | tf_op jit(solution)/shard_map/pallas_call | solution.py:537
  6.8 0.0 collective-permute-done.r_odd
  6.8 0.0 collective-permute-done.1.r_even
  6.8 0.7 %shard_map.78 = (bf16[8,48,128]{2,1,0:T(8,128)(2,1)S(1)}, bf16[8,48,128]{2,1,0:T(8,128)(2,1)S(1)}) custom-call(bf16[8,48,128]{2,1,0:T(8,128)(2,1)S(1)} %collective-permute-done.r_odd, bf16[8,48,128]{2,1,0:T(8,128)(2,1)S(1)} %collective-permute-done.1.r_even, bf16[16,16,512]{2,1,0:T(8,128)(2,1)S(1)} %get-tuple-element.30.msk, ...), custom_call_target="tpu_custom_call" | custom-call | flops 10000000 | bytes 1048576 | tf_op jit(solution)/shard_map/pallas_call | solution.py:537
  7.5 1.9 %collective-permute-start.2 = (bf16[8,48,128]{2,1,0:T(8,128)(2,1)S(1)}, bf16[8,48,128]{2,1,0:T(8,128)(2,1)S(1)}, u32[]{:S(2)}, u32[]{:S(2)}) collective-permute-start(bf16[8,48,128]{2,1,0:T(8,128)(2,1)S(1)} %get-tuple-element.51), channel_id=1, source_target_pairs={{0,8},{1,9},{2,10},{3,11},{4,12},{5,13},{6,14},{7,15},{8,0},{9,1},... | collective-permute-start | bytes 294920 | tf_op jit(solution)/shard_map/ppermute | solution.py:555
  9.5 2.8 %collective-permute-start.3 = (bf16[8,48,128]{2,1,0:T(8,128)(2,1)S(1)}, bf16[8,48,128]{2,1,0:T(8,128)(2,1)S(1)}, u32[]{:S(2)}, u32[]{:S(2)}) collective-permute-start(bf16[8,48,128]{2,1,0:T(8,128)(2,1)S(1)} %get-tuple-element.52), channel_id=1, source_target_pairs={{0,1},{1,0},{2,3},{3,2},{4,5},{5,4},{6,7},{7,6},{8,16},{9,17},{10,... | collective-permute-start | bytes 294920 | tf_op jit(solution)/shard_map/ppermute | solution.py:555
  12.3 0.0 slice-done
  12.3 0.0 slice-done.1
  12.3 0.0 copy-start.3
  12.3 3.8 %shard_map.77 = (f32[8,256,128]{2,1,0:T(8,128)S(1)}, f32[4,256,128]{2,1,0:T(8,128)S(1)}, f32[8,64,128]{2,1,0:T(8,128)S(1)}, f32[8,32,128]{2,1,0:T(8,128)S(1)}, f32[8,16,128]{2,1,0:T(8,128)S(1)}) custom-call(bf16[8,48,128]{2,1,0:T(8,128)(2,1)S(1)} %collective-permute-done.r_odd, bf16[8,48,128]{2,1,0:T(8,128)(2,1)S(1)} %collective-permute-done.1.r_even, ...), custom_call_target="tpu_custom_call" | custom-call | flops 1000000000 | bytes 1048576 | tf_op jit(solution)/shard_map/pallas_call | solution.py:537
  16.1 0.0 collective-permute-done.2.x_even
  16.1 0.1 collective-permute-done.3.x_odd
  16.2 0.0 copy-done.3
  16.2 2.3 %shard_map.79 = bf16[16,16,512]{2,1,0:T(8,128)(2,1)} custom-call(f32[256,128]{1,0:T(8,128)S(1)} %get-tuple-element.29.count, f32[8,256,128]{2,1,0:T(8,128)S(1)} %get-tuple-element.46.inc0, f32[4,256,128]{2,1,0:T(8,128)S(1)} %get-tuple-element.47.near_base, f32[8,64,128]{2,1,0:T(8,128)S(1)} %get-tuple-element.48.own1, ...), custom_call_target="tpu_custom_call" | custom-call | flops 3000000000 | bytes 1048576 | tf_op jit(solution)/shard_map/pallas_call | solution.py:537
  (1 shorter events, 0.0 us)
Async XLA Ops:
  0.0 0.9 %copy-start.1 = (bf16[16,16,512]{2,1,0:T(8,128)(2,1)S(1)}, bf16[16,16,512]{2,1,0:T(8,128)(2,1)}, u32[]{:S(2)}) copy-start(bf16[16,16,512]{2,1,0:T(8,128)(2,1)} %cur.1) | copy-start | bytes 786436
  0.0 1.0 %copy-start.2 = (s32[16,16]{1,0:T(8,128)S(1)}, s32[16,16]{1,0:T(8,128)}, u32[]{:S(2)}) copy-start(s32[16,16]{1,0:T(8,128)} %cnt.1) | copy-start | bytes 3076
  0.0 1.3 %copy-start = (bf16[512,1024]{1,0:T(8,128)(2,1)S(1)}, bf16[512,1024]{1,0:T(8,128)(2,1)}, u32[]{:S(2)}) copy-start(bf16[512,1024]{1,0:T(8,128)(2,1)} %rad.5) | copy-start | bytes 3145732
  0.0 1.3 %copy-start.5 = (f32[3,4,1024]{2,1,0:T(4,128)S(1)}, f32[3,4,1024]{2,1,0:T(4,128)}, u32[]{:S(2)}) copy-start(f32[3,4,1024]{2,1,0:T(4,128)} %shf.3) | copy-start | bytes 147460
  1.3 2.8 %copy-start.4 = (f32[4,49,1024]{2,0,1:T(4,128)S(1)}, f32[4,49,1024]{2,0,1:T(4,128)}, u32[]{:S(2)}) copy-start(f32[4,49,1024]{2,0,1:T(4,128)} %param.12) | copy-start | bytes 2408452
  2.1 4.7 %collective-permute-start = (bf16[8,48,128]{2,1,0:T(8,128)(2,1)S(1)}, bf16[8,48,128]{2,1,0:T(8,128)(2,1)S(1)}, u32[]{:S(2)}, u32[]{:S(2)}) collective-permute-start(bf16[8,48,128]{2,1,0:T(8,128)(2,1)S(1)} %get-tuple-element.32), channel_id=1, source_target_pairs={{0,8},{1,2},{2,1},{3,4},{4,3},{5,6},{6,5},{7,15},{8,0},{9,10},{10,... | collective-permute-start | bytes 294920 | tf_op jit(solution)/shard_map/ppermute | solution.py:555
  4.1 2.7 %collective-permute-start.1 = (bf16[8,48,128]{2,1,0:T(8,128)(2,1)S(1)}, bf16[8,48,128]{2,1,0:T(8,128)(2,1)S(1)}, u32[]{:S(2)}, u32[]{:S(2)}) collective-permute-start(bf16[8,48,128]{2,1,0:T(8,128)(2,1)S(1)} %get-tuple-element.33), channel_id=1, source_target_pairs={{0,1},{1,0},{2,3},{3,2},{4,5},{5,4},{6,7},{7,6},{8,9},{9,8},{10,11... | collective-permute-start | bytes 294920 | tf_op jit(solution)/shard_map/ppermute | solution.py:555
  4.1 8.2 %slice-start = ((s8[4718592]{0:T(1024)(128)(4,1)}), s8[4194304]{0:T(1024)(128)(4,1)S(1)}, s32[]{:S(2)}) async-start(s8[4718592]{0:T(1024)(128)(4,1)} %bitcast.1), calls=%async_computation | async-start | bytes 8388608
  4.1 8.2 %slice-start.1 = ((s8[4718592]{0:T(1024)(128)(4,1)}), s8[524288]{0:T(1024)(128)(4,1)S(1)}, s32[]{:S(2)}) async-start(s8[4718592]{0:T(1024)(128)(4,1)} %bitcast.1), calls=%async_computation.1 | async-start | bytes 1048576
  7.5 8.5 %collective-permute-start.2 = (bf16[8,48,128]{2,1,0:T(8,128)(2,1)S(1)}, bf16[8,48,128]{2,1,0:T(8,128)(2,1)S(1)}, u32[]{:S(2)}, u32[]{:S(2)}) collective-permute-start(bf16[8,48,128]{2,1,0:T(8,128)(2,1)S(1)} %get-tuple-element.51), channel_id=1, source_target_pairs={{0,8},{1,9},{2,10},{3,11},{4,12},{5,13},{6,14},{7,15},{8,0},{9,1},... | collective-permute-start | bytes 294920 | tf_op jit(solution)/shard_map/ppermute | solution.py:555
  9.5 6.7 %collective-permute-start.3 = (bf16[8,48,128]{2,1,0:T(8,128)(2,1)S(1)}, bf16[8,48,128]{2,1,0:T(8,128)(2,1)S(1)}, u32[]{:S(2)}, u32[]{:S(2)}) collective-permute-start(bf16[8,48,128]{2,1,0:T(8,128)(2,1)S(1)} %get-tuple-element.52), channel_id=1, source_target_pairs={{0,1},{1,0},{2,3},{3,2},{4,5},{5,4},{6,7},{7,6},{8,16},{9,17},{10,... | collective-permute-start | bytes 294920 | tf_op jit(solution)/shard_map/ppermute | solution.py:555
  12.3 3.9 %copy-start.3 = (bf16[1024,512]{1,0:T(8,128)(2,1)S(1)}, bf16[1024,512]{1,0:T(8,128)(2,1)}, u32[]{:S(2)}) copy-start(bf16[1024,512]{1,0:T(8,128)(2,1)} %rec.1) | copy-start | bytes 3145732
